TPU v7x, 256 devices: a whole 4x4x8 slice. The times are simulated.
256 devices in a mesh: dp: 8 (over y, x_hi), seq: 32 (over x_lo, z, core).
Axes of the slice: x: 4 (x_hi: 2, x_lo: 2; x = x_hi * 2 + x_lo), y: 4, z: 8, core: 2. Of those that a mesh axis runs over, the one named last changes fastest.
Arguments:
- frames_in: bfloat16 [65536, 1536], P(('dp', 'seq')), parts along dimension 0, may hold values from -3 to 3
- queries: bfloat16 [65536, 768], P(('dp', 'seq')), parts along dimension 0, may hold values from -24 to 24
- keys: bfloat16 [65536, 768], P(('dp', 'seq')), parts along dimension 0, may hold values from -6 to 6
- values: bfloat16 [65536, 768], P(('dp', 'seq')), parts along dimension 0, may hold values from -6 to 6
- w_out: bfloat16 [768, 1536], replicated, may hold values from -0.21875 to 0.21875
- ln_gain: float32 [1536], replicated, may hold values from 0.5 to 1.5
- w_glu: bfloat16 [1536, 1536], replicated, may hold values from -0.15625 to 0.15625
- dw_weight: float32 [31, 768], replicated, may hold values from -1 to 1
- bn_scale: float32 [768], replicated, may hold values from 0.5 to 2
- bn_shift: float32 [768], replicated, may hold values from -2 to 2
Outputs:
- attended: bfloat16 [65536, 1536], P(('dp', 'seq')), parts along dimension 0
- conv_out: bfloat16 [65536, 768], P(('dp', 'seq')), parts along dimension 0
There are 8 independent parts, one for each index of `dp`. A program takes and returns all parts, laid end to end along the dimension named above; an argument that names none is the same for every part. Nothing has to cross between parts.
All inputs are finite; a program needn't handle non-finite values.
Results may differ from a plain program's by a relative error of at most 0.013.
Values may be sent and summed in bfloat16 or wider, within the bound.
A program may use at most 128 MiB of HBM per device.

v0:
```python
import math

import jax
import jax.numpy as jnp
from jax import lax
from jax.sharding import PartitionSpec as P

HD = 64
TAPS = 31


def with_halo(block, sides, width):
    for axis, dim in sides:
        count = lax.axis_size(axis)
        forward = [(i, i + 1) for i in range(count - 1)]
        backward = [(target, source) for source, target in forward]
        low = lax.ppermute(
            lax.slice_in_dim(block, block.shape[dim] - width, None, axis=dim), axis, forward
        )
        high = lax.ppermute(lax.slice_in_dim(block, 0, width, axis=dim), axis, backward)
        block = jnp.concatenate([low, block, high], axis=dim)
    return block


def attend_block(query_heads, carry, key_block, value_block):
    running_max, weight_sum, accumulated = carry
    scale = 1.0 / math.sqrt(HD)
    scores = (
        jnp.einsum("qhd,khd->hqk", query_heads, key_block, preferred_element_type=jnp.float32)
        * scale
    )
    new_max = jnp.maximum(running_max, jnp.max(scores, axis=2))
    weights = jnp.exp(scores - new_max[:, :, None])
    correction = jnp.exp(running_max - new_max)
    weight_sum = weight_sum * correction + jnp.sum(weights, axis=2)
    product = jnp.einsum(
        "hqk,khd->qhd",
        weights.astype(jnp.bfloat16),
        value_block,
        preferred_element_type=jnp.float32,
    )
    accumulated = accumulated * correction.T[:, :, None] + product
    return (new_max, weight_sum, accumulated)


def fold_keys(query_heads, carry, key_split, value_split):
    count = key_split.shape[0]
    block = math.gcd(count, 512)
    key_blocks = key_split.reshape(count // block, block, key_split.shape[1], HD)
    value_blocks = value_split.reshape(count // block, block, key_split.shape[1], HD)

    def scan_step(state, pair):
        return (attend_block(query_heads, state, pair[0], pair[1]), None)

    carry, unused = lax.scan(scan_step, carry, (key_blocks, value_blocks))
    return carry


def start_state(head_count, rows):
    return (
        jnp.full((head_count, rows), -1e30, jnp.float32),
        jnp.zeros((head_count, rows), jnp.float32),
        jnp.zeros((rows, head_count, HD), jnp.float32),
    )


def finish_state(state):
    running_max, weight_sum, accumulated = state
    return accumulated / weight_sum.T[:, :, None]


def local(frames_in, queries, keys, values, w_out, ln_gain, w_glu, dw_weight, bn_scale, bn_shift):
    local_rows = queries.shape[0]
    head_count = queries.shape[1] // HD
    channels = w_glu.shape[1] // 2
    query_heads = queries.reshape(local_rows, head_count, HD)
    initial = start_state(head_count, local_rows)
    key_piece = lax.all_gather(keys, "seq", axis=0, tiled=True)
    value_piece = lax.all_gather(values, "seq", axis=0, tiled=True)
    count = key_piece.shape[0]
    final_state = fold_keys(
        query_heads,
        initial,
        key_piece.reshape(count, head_count, HD),
        value_piece.reshape(count, head_count, HD),
    )
    context = finish_state(final_state).reshape(local_rows, head_count * HD).astype(jnp.bfloat16)
    residual_sum = frames_in.astype(jnp.float32) + jnp.dot(
        context, w_out, preferred_element_type=jnp.float32
    )
    attended = residual_sum.astype(jnp.bfloat16)
    mean_value = jnp.mean(residual_sum, axis=1, keepdims=True)
    centered = residual_sum - mean_value
    variance = jnp.mean(centered * centered, axis=1, keepdims=True)
    normed = (centered / jnp.sqrt(variance + 1e-05) * ln_gain).astype(jnp.bfloat16)
    projected = jnp.dot(normed, w_glu, preferred_element_type=jnp.float32)
    gated = (projected[:, :channels] * jax.nn.sigmoid(projected[:, channels:])).astype(jnp.bfloat16)
    half_width = TAPS // 2
    padded = with_halo(gated, (("seq", 0),), half_width)
    conv = jnp.zeros((local_rows, channels), jnp.float32)
    for tap_index in range(TAPS):
        conv = (
            conv
            + padded[tap_index : tap_index + local_rows].astype(jnp.float32) * dw_weight[tap_index]
        )
    shifted = bn_scale * conv + bn_shift
    conv_out = (shifted * jax.nn.sigmoid(shifted)).astype(jnp.bfloat16)
    return (attended, conv_out)


def solution(mesh):
    placed = (
        P(("dp", "seq"), None),
        P(("dp", "seq"), None),
        P(("dp", "seq"), None),
        P(("dp", "seq"), None),
        P(),
        P(),
        P(),
        P(),
        P(),
        P(),
    )
    return jax.shard_map(
        local,
        mesh=mesh,
        in_specs=placed,
        out_specs=(P(("dp", "seq"), None), P(("dp", "seq"), None)),
        check_vma=False,
    )
```

profile of v0, /device:TPU:1, one launch (start us, length us, event | category | flops | bytes accessed | tf_op | source)
XLA Modules:
  0.0 453.4 jit_solution(14224835474146481990)
XLA Ops:
  12.0 82.2 %all-gather.3.cloned.1.call-done = bf16[8192,768]{1,0:T(8,128)(2,1)} async-done(((bf16[256,768]{1,0:T(8,128)(2,1)}), bf16[8192,768]{1,0:T(8,128)(2,1)}) %all-gather.3.cloned.1.call-update) | async-done | bytes 12582928 | tf_op jit(solution)/shard_map/all_gather | solution.py:78
  94.1 16.0 %copy.15 = bf16[8192,768]{0,1:T(8,128)(2,1)} copy(bf16[8192,768]{1,0:T(8,128)(2,1)} %all-gather.3.cloned.1.call-done) | data formatting | bytes 25165824 | tf_op jit(solution)/shard_map/all_gather | solution.py:78
  110.2 9.5 %copy.21 = bf16[96,8,16,512]{3,2,1,0:T(8,128)(2,1)S(1)} copy(bf16[96,8,16,512]{3,1,2,0:T(8,128)(2,1)} %bitcast.61) | data formatting | bytes 25165824
  119.7 18.6 %copy.18 = bf16[16,512,12,64]{1,3,2,0:T(8,128)(2,1)} copy(bf16[16,512,12,64]{1,0,3,2:T(8,128)(2,1)S(1)} %bitcast.62) | data formatting | bytes 25165824
  138.3 37.7 %all-gather.5.cloned.1.call-done = bf16[8192,768]{1,0:T(8,128)(2,1)} async-done(((bf16[256,768]{1,0:T(8,128)(2,1)}), bf16[8192,768]{1,0:T(8,128)(2,1)}) %all-gather.5.cloned.1.call-update) | async-done | bytes 12582928 | tf_op jit(solution)/shard_map/all_gather | solution.py:79
  176.0 16.0 %copy.17 = bf16[8192,768]{0,1:T(8,128)(2,1)} copy(bf16[8192,768]{1,0:T(8,128)(2,1)} %all-gather.5.cloned.1.call-done) | data formatting | bytes 25165824 | tf_op jit(solution)/shard_map/all_gather | solution.py:79
  192.1 9.4 %copy.22 = bf16[96,8,16,512]{3,2,1,0:T(8,128)(2,1)S(1)} copy(bf16[96,8,16,512]{3,1,2,0:T(8,128)(2,1)} %bitcast.63) | data formatting | bytes 25165824
  201.5 18.6 %copy.19 = bf16[16,512,12,64]{1,3,2,0:T(8,128)(2,1)} copy(bf16[16,512,12,64]{1,0,3,2:T(8,128)(2,1)S(1)} %bitcast.64) | data formatting | bytes 25165824
  220.1 205.0 %while.15 = (s32[]{:T(128)}, f32[12,256]{1,0:T(8,128)}, f32[12,256]{1,0:T(8,128)}, f32[256,12,64]{0,2,1:T(8,128)S(1)}, bf16[16,512,12,64]{1,3,2,0:T(8,128)(2,1)}...) while((s32[]{:T(128)}, f32[12,256]{1,0:T(8,128)}, ...), condition=%wide.region_3.4_spmd.clone, body=%wide.region_0.3_spmd.clone.sunk | while | flops 415844352 | bytes 47924436 | solution.py:55
  220.1 4.9 %bitcast_reduce_fusion.2 = (f32[12,256]{1,0:T(8,128)S(1)}, f32[12,512,256]{2,1,0:T(8,128)}) fusion(bf16[256,12,64]{0,2,1:T(8,128)(2,1)S(1)} %get-tuple-element.202, bf16[16,512,12,64]{1,3,2,0:T(8,128)(2,1)} %get-tuple-element.201, s32[]{:T(128)} %get-tuple-element.188), kind=kOutput, calls=%fused_computation.1.clone.1 | convolution fusion | flops 204469248 | bytes 7483904 | tf_op jit(solution)/shard_map/while/body/eval_jaxpr/qhd,khd->hqk/dot_general | solution.py:29
  232.1 4.9 %bitcast_reduce_fusion.2 = (f32[12,256]{1,0:T(8,128)S(1)}, f32[12,512,256]{2,1,0:T(8,128)}) fusion(bf16[256,12,64]{0,2,1:T(8,128)(2,1)S(1)} %get-tuple-element.202, bf16[16,512,12,64]{1,3,2,0:T(8,128)(2,1)} %get-tuple-element.201, s32[]{:T(128)} %get-tuple-element.188), kind=kOutput, calls=%fused_computation.1.clone.1 | convolution fusion | flops 204469248 | bytes 7483904 | tf_op jit(solution)/shard_map/while/body/eval_jaxpr/qhd,khd->hqk/dot_general | solution.py:29
  245.0 4.9 %bitcast_reduce_fusion.2 = (f32[12,256]{1,0:T(8,128)S(1)}, f32[12,512,256]{2,1,0:T(8,128)}) fusion(bf16[256,12,64]{0,2,1:T(8,128)(2,1)S(1)} %get-tuple-element.202, bf16[16,512,12,64]{1,3,2,0:T(8,128)(2,1)} %get-tuple-element.201, s32[]{:T(128)} %get-tuple-element.188), kind=kOutput, calls=%fused_computation.1.clone.1 | convolution fusion | flops 204469248 | bytes 7483904 | tf_op jit(solution)/shard_map/while/body/eval_jaxpr/qhd,khd->hqk/dot_general | solution.py:29
  250.7 4.8 %fusion.79 = f32[256,12,64]{0,2,1:T(8,128)S(1)} fusion(f32[12,512,256]{2,1,0:T(8,128)} %get-tuple-element.177, f32[12,256]{1,0:T(8,128)S(1)} %get-tuple-element.198, f32[256,12,64]{0,2,1:T(8,128)S(1)} %get-tuple-element.191, bf16[16,512,12,64]{1,3,2,0:T(8,128)(2,1)} %get-tuple-element.203, s32[]{:T(128)} %get-tuple-element.188, ...), kind=kOutput, calls=%fused_computation.9.clone.1 | convolution fusion | flops 206635008 | bytes 8675841 | tf_op jit(solution)/shard_map/while/body/eval_jaxpr/hqk,khd->qhd/dot_general | solution.py:36
  257.8 4.9 %bitcast_reduce_fusion.2 = (f32[12,256]{1,0:T(8,128)S(1)}, f32[12,512,256]{2,1,0:T(8,128)}) fusion(bf16[256,12,64]{0,2,1:T(8,128)(2,1)S(1)} %get-tuple-element.202, bf16[16,512,12,64]{1,3,2,0:T(8,128)(2,1)} %get-tuple-element.201, s32[]{:T(128)} %get-tuple-element.188), kind=kOutput, calls=%fused_computation.1.clone.1 | convolution fusion | flops 204469248 | bytes 7483904 | tf_op jit(solution)/shard_map/while/body/eval_jaxpr/qhd,khd->hqk/dot_general | solution.py:29
  270.7 4.9 %bitcast_reduce_fusion.2 = (f32[12,256]{1,0:T(8,128)S(1)}, f32[12,512,256]{2,1,0:T(8,128)}) fusion(bf16[256,12,64]{0,2,1:T(8,128)(2,1)S(1)} %get-tuple-element.202, bf16[16,512,12,64]{1,3,2,0:T(8,128)(2,1)} %get-tuple-element.201, s32[]{:T(128)} %get-tuple-element.188), kind=kOutput, calls=%fused_computation.1.clone.1 | convolution fusion | flops 204469248 | bytes 7483904 | tf_op jit(solution)/shard_map/while/body/eval_jaxpr/qhd,khd->hqk/dot_general | solution.py:29
  283.6 4.9 %bitcast_reduce_fusion.2 = (f32[12,256]{1,0:T(8,128)S(1)}, f32[12,512,256]{2,1,0:T(8,128)}) fusion(bf16[256,12,64]{0,2,1:T(8,128)(2,1)S(1)} %get-tuple-element.202, bf16[16,512,12,64]{1,3,2,0:T(8,128)(2,1)} %get-tuple-element.201, s32[]{:T(128)} %get-tuple-element.188), kind=kOutput, calls=%fused_computation.1.clone.1 | convolution fusion | flops 204469248 | bytes 7483904 | tf_op jit(solution)/shard_map/while/body/eval_jaxpr/qhd,khd->hqk/dot_general | solution.py:29
  289.3 4.8 %fusion.79 = f32[256,12,64]{0,2,1:T(8,128)S(1)} fusion(f32[12,512,256]{2,1,0:T(8,128)} %get-tuple-element.177, f32[12,256]{1,0:T(8,128)S(1)} %get-tuple-element.198, f32[256,12,64]{0,2,1:T(8,128)S(1)} %get-tuple-element.191, bf16[16,512,12,64]{1,3,2,0:T(8,128)(2,1)} %get-tuple-element.203, s32[]{:T(128)} %get-tuple-element.188, ...), kind=kOutput, calls=%fused_computation.9.clone.1 | convolution fusion | flops 206635008 | bytes 8675841 | tf_op jit(solution)/shard_map/while/body/eval_jaxpr/hqk,khd->qhd/dot_general | solution.py:36
  296.4 4.9 %bitcast_reduce_fusion.2 = (f32[12,256]{1,0:T(8,128)S(1)}, f32[12,512,256]{2,1,0:T(8,128)}) fusion(bf16[256,12,64]{0,2,1:T(8,128)(2,1)S(1)} %get-tuple-element.202, bf16[16,512,12,64]{1,3,2,0:T(8,128)(2,1)} %get-tuple-element.201, s32[]{:T(128)} %get-tuple-element.188), kind=kOutput, calls=%fused_computation.1.clone.1 | convolution fusion | flops 204469248 | bytes 7483904 | tf_op jit(solution)/shard_map/while/body/eval_jaxpr/qhd,khd->hqk/dot_general | solution.py:29
  309.3 4.9 %bitcast_reduce_fusion.2 = (f32[12,256]{1,0:T(8,128)S(1)}, f32[12,512,256]{2,1,0:T(8,128)}) fusion(bf16[256,12,64]{0,2,1:T(8,128)(2,1)S(1)} %get-tuple-element.202, bf16[16,512,12,64]{1,3,2,0:T(8,128)(2,1)} %get-tuple-element.201, s32[]{:T(128)} %get-tuple-element.188), kind=kOutput, calls=%fused_computation.1.clone.1 | convolution fusion | flops 204469248 | bytes 7483904 | tf_op jit(solution)/shard_map/while/body/eval_jaxpr/qhd,khd->hqk/dot_general | solution.py:29
  315.1 4.8 %fusion.79 = f32[256,12,64]{0,2,1:T(8,128)S(1)} fusion(f32[12,512,256]{2,1,0:T(8,128)} %get-tuple-element.177, f32[12,256]{1,0:T(8,128)S(1)} %get-tuple-element.198, f32[256,12,64]{0,2,1:T(8,128)S(1)} %get-tuple-element.191, bf16[16,512,12,64]{1,3,2,0:T(8,128)(2,1)} %get-tuple-element.203, s32[]{:T(128)} %get-tuple-element.188, ...), kind=kOutput, calls=%fused_computation.9.clone.1 | convolution fusion | flops 206635008 | bytes 8675841 | tf_op jit(solution)/shard_map/while/body/eval_jaxpr/hqk,khd->qhd/dot_general | solution.py:36
  322.1 4.9 %bitcast_reduce_fusion.2 = (f32[12,256]{1,0:T(8,128)S(1)}, f32[12,512,256]{2,1,0:T(8,128)}) fusion(bf16[256,12,64]{0,2,1:T(8,128)(2,1)S(1)} %get-tuple-element.202, bf16[16,512,12,64]{1,3,2,0:T(8,128)(2,1)} %get-tuple-element.201, s32[]{:T(128)} %get-tuple-element.188), kind=kOutput, calls=%fused_computation.1.clone.1 | convolution fusion | flops 204469248 | bytes 7483904 | tf_op jit(solution)/shard_map/while/body/eval_jaxpr/qhd,khd->hqk/dot_general | solution.py:29
  327.9 4.8 %fusion.79 = f32[256,12,64]{0,2,1:T(8,128)S(1)} fusion(f32[12,512,256]{2,1,0:T(8,128)} %get-tuple-element.177, f32[12,256]{1,0:T(8,128)S(1)} %get-tuple-element.198, f32[256,12,64]{0,2,1:T(8,128)S(1)} %get-tuple-element.191, bf16[16,512,12,64]{1,3,2,0:T(8,128)(2,1)} %get-tuple-element.203, s32[]{:T(128)} %get-tuple-element.188, ...), kind=kOutput, calls=%fused_computation.9.clone.1 | convolution fusion | flops 206635008 | bytes 8675841 | tf_op jit(solution)/shard_map/while/body/eval_jaxpr/hqk,khd->qhd/dot_general | solution.py:36
  335.0 4.9 %bitcast_reduce_fusion.2 = (f32[12,256]{1,0:T(8,128)S(1)}, f32[12,512,256]{2,1,0:T(8,128)}) fusion(bf16[256,12,64]{0,2,1:T(8,128)(2,1)S(1)} %get-tuple-element.202, bf16[16,512,12,64]{1,3,2,0:T(8,128)(2,1)} %get-tuple-element.201, s32[]{:T(128)} %get-tuple-element.188), kind=kOutput, calls=%fused_computation.1.clone.1 | convolution fusion | flops 204469248 | bytes 7483904 | tf_op jit(solution)/shard_map/while/body/eval_jaxpr/qhd,khd->hqk/dot_general | solution.py:29
  340.8 4.8 %fusion.79 = f32[256,12,64]{0,2,1:T(8,128)S(1)} fusion(f32[12,512,256]{2,1,0:T(8,128)} %get-tuple-element.177, f32[12,256]{1,0:T(8,128)S(1)} %get-tuple-element.198, f32[256,12,64]{0,2,1:T(8,128)S(1)} %get-tuple-element.191, bf16[16,512,12,64]{1,3,2,0:T(8,128)(2,1)} %get-tuple-element.203, s32[]{:T(128)} %get-tuple-element.188, ...), kind=kOutput, calls=%fused_computation.9.clone.1 | convolution fusion | flops 206635008 | bytes 8675841 | tf_op jit(solution)/shard_map/while/body/eval_jaxpr/hqk,khd->qhd/dot_general | solution.py:36
  347.9 4.9 %bitcast_reduce_fusion.2 = (f32[12,256]{1,0:T(8,128)S(1)}, f32[12,512,256]{2,1,0:T(8,128)}) fusion(bf16[256,12,64]{0,2,1:T(8,128)(2,1)S(1)} %get-tuple-element.202, bf16[16,512,12,64]{1,3,2,0:T(8,128)(2,1)} %get-tuple-element.201, s32[]{:T(128)} %get-tuple-element.188), kind=kOutput, calls=%fused_computation.1.clone.1 | convolution fusion | flops 204469248 | bytes 7483904 | tf_op jit(solution)/shard_map/while/body/eval_jaxpr/qhd,khd->hqk/dot_general | solution.py:29
  353.7 4.8 %fusion.79 = f32[256,12,64]{0,2,1:T(8,128)S(1)} fusion(f32[12,512,256]{2,1,0:T(8,128)} %get-tuple-element.177, f32[12,256]{1,0:T(8,128)S(1)} %get-tuple-element.198, f32[256,12,64]{0,2,1:T(8,128)S(1)} %get-tuple-element.191, bf16[16,512,12,64]{1,3,2,0:T(8,128)(2,1)} %get-tuple-element.203, s32[]{:T(128)} %get-tuple-element.188, ...), kind=kOutput, calls=%fused_computation.9.clone.1 | convolution fusion | flops 206635008 | bytes 8675841 | tf_op jit(solution)/shard_map/while/body/eval_jaxpr/hqk,khd->qhd/dot_general | solution.py:36
  360.7 4.9 %bitcast_reduce_fusion.2 = (f32[12,256]{1,0:T(8,128)S(1)}, f32[12,512,256]{2,1,0:T(8,128)}) fusion(bf16[256,12,64]{0,2,1:T(8,128)(2,1)S(1)} %get-tuple-element.202, bf16[16,512,12,64]{1,3,2,0:T(8,128)(2,1)} %get-tuple-element.201, s32[]{:T(128)} %get-tuple-element.188), kind=kOutput, calls=%fused_computation.1.clone.1 | convolution fusion | flops 204469248 | bytes 7483904 | tf_op jit(solution)/shard_map/while/body/eval_jaxpr/qhd,khd->hqk/dot_general | solution.py:29
  373.6 4.9 %bitcast_reduce_fusion.2 = (f32[12,256]{1,0:T(8,128)S(1)}, f32[12,512,256]{2,1,0:T(8,128)}) fusion(bf16[256,12,64]{0,2,1:T(8,128)(2,1)S(1)} %get-tuple-element.202, bf16[16,512,12,64]{1,3,2,0:T(8,128)(2,1)} %get-tuple-element.201, s32[]{:T(128)} %get-tuple-element.188), kind=kOutput, calls=%fused_computation.1.clone.1 | convolution fusion | flops 204469248 | bytes 7483904 | tf_op jit(solution)/shard_map/while/body/eval_jaxpr/qhd,khd->hqk/dot_general | solution.py:29
  379.4 4.8 %fusion.79 = f32[256,12,64]{0,2,1:T(8,128)S(1)} fusion(f32[12,512,256]{2,1,0:T(8,128)} %get-tuple-element.177, f32[12,256]{1,0:T(8,128)S(1)} %get-tuple-element.198, f32[256,12,64]{0,2,1:T(8,128)S(1)} %get-tuple-element.191, bf16[16,512,12,64]{1,3,2,0:T(8,128)(2,1)} %get-tuple-element.203, s32[]{:T(128)} %get-tuple-element.188, ...), kind=kOutput, calls=%fused_computation.9.clone.1 | convolution fusion | flops 206635008 | bytes 8675841 | tf_op jit(solution)/shard_map/while/body/eval_jaxpr/hqk,khd->qhd/dot_general | solution.py:36
  386.5 4.9 %bitcast_reduce_fusion.2 = (f32[12,256]{1,0:T(8,128)S(1)}, f32[12,512,256]{2,1,0:T(8,128)}) fusion(bf16[256,12,64]{0,2,1:T(8,128)(2,1)S(1)} %get-tuple-element.202, bf16[16,512,12,64]{1,3,2,0:T(8,128)(2,1)} %get-tuple-element.201, s32[]{:T(128)} %get-tuple-element.188), kind=kOutput, calls=%fused_computation.1.clone.1 | convolution fusion | flops 204469248 | bytes 7483904 | tf_op jit(solution)/shard_map/while/body/eval_jaxpr/qhd,khd->hqk/dot_general | solution.py:29
  399.3 4.9 %bitcast_reduce_fusion.2 = (f32[12,256]{1,0:T(8,128)S(1)}, f32[12,512,256]{2,1,0:T(8,128)}) fusion(bf16[256,12,64]{0,2,1:T(8,128)(2,1)S(1)} %get-tuple-element.202, bf16[16,512,12,64]{1,3,2,0:T(8,128)(2,1)} %get-tuple-element.201, s32[]{:T(128)} %get-tuple-element.188), kind=kOutput, calls=%fused_computation.1.clone.1 | convolution fusion | flops 204469248 | bytes 7483904 | tf_op jit(solution)/shard_map/while/body/eval_jaxpr/qhd,khd->hqk/dot_general | solution.py:29
  412.2 4.9 %bitcast_reduce_fusion.2 = (f32[12,256]{1,0:T(8,128)S(1)}, f32[12,512,256]{2,1,0:T(8,128)}) fusion(bf16[256,12,64]{0,2,1:T(8,128)(2,1)S(1)} %get-tuple-element.202, bf16[16,512,12,64]{1,3,2,0:T(8,128)(2,1)} %get-tuple-element.201, s32[]{:T(128)} %get-tuple-element.188), kind=kOutput, calls=%fused_computation.1.clone.1 | convolution fusion | flops 204469248 | bytes 7483904 | tf_op jit(solution)/shard_map/while/body/eval_jaxpr/qhd,khd->hqk/dot_general | solution.py:29
  (270 shorter events, 118.3 us)
Async XLA Ops:
  7.2 418.7 %copy-start = (bf16[768,1536]{1,0:T(8,128)(2,1)S(1)}, bf16[768,1536]{1,0:T(8,128)(2,1)}, u32[]{:S(2)}) copy-start(bf16[768,1536]{1,0:T(8,128)(2,1)} %param.16) | copy-start | bytes 7077892
  7.2 87.0 %all-gather.3.cloned.1.call-start = ((), (), s32[]{:S(2)}) async-start(), calls=%async_computation | async-start | bytes 12976128 | tf_op jit(solution)/shard_map/all_gather | solution.py:78
  7.9 168.1 %all-gather.5.cloned.1.call-start = ((), (), s32[]{:S(2)}) async-start(), calls=%async_computation.1 | async-start | bytes 12976128 | tf_op jit(solution)/shard_map/all_gather | solution.py:79
  237.9 5.8 %copy-start.2 = (f32[12,256]{1,0:T(8,128)S(1)}, f32[12,256]{1,0:T(8,128)}, u32[]{:S(2)}) copy-start(f32[12,256]{1,0:T(8,128)} %get-tuple-element.189) | copy-start | bytes 36868 | tf_op jit(solution)/shard_map/while
  250.7 5.8 %copy-start.2 = (f32[12,256]{1,0:T(8,128)S(1)}, f32[12,256]{1,0:T(8,128)}, u32[]{:S(2)}) copy-start(f32[12,256]{1,0:T(8,128)} %get-tuple-element.189) | copy-start | bytes 36868 | tf_op jit(solution)/shard_map/while
  263.6 5.8 %copy-start.2 = (f32[12,256]{1,0:T(8,128)S(1)}, f32[12,256]{1,0:T(8,128)}, u32[]{:S(2)}) copy-start(f32[12,256]{1,0:T(8,128)} %get-tuple-element.189) | copy-start | bytes 36868 | tf_op jit(solution)/shard_map/while
  276.5 5.8 %copy-start.2 = (f32[12,256]{1,0:T(8,128)S(1)}, f32[12,256]{1,0:T(8,128)}, u32[]{:S(2)}) copy-start(f32[12,256]{1,0:T(8,128)} %get-tuple-element.189) | copy-start | bytes 36868 | tf_op jit(solution)/shard_map/while
  289.3 5.8 %copy-start.2 = (f32[12,256]{1,0:T(8,128)S(1)}, f32[12,256]{1,0:T(8,128)}, u32[]{:S(2)}) copy-start(f32[12,256]{1,0:T(8,128)} %get-tuple-element.189) | copy-start | bytes 36868 | tf_op jit(solution)/shard_map/while
  302.2 5.8 %copy-start.2 = (f32[12,256]{1,0:T(8,128)S(1)}, f32[12,256]{1,0:T(8,128)}, u32[]{:S(2)}) copy-start(f32[12,256]{1,0:T(8,128)} %get-tuple-element.189) | copy-start | bytes 36868 | tf_op jit(solution)/shard_map/while
  429.1 12.8 %copy-start.5 = (f32[768]{0:T(1024)S(1)}, f32[768]{0:T(1024)}, u32[]{:S(2)}) copy-start(f32[768]{0:T(1024)} %get-tuple-element.73) | copy-start | bytes 9220
  429.1 12.8 %copy-start.6 = (f32[768]{0:T(1024)S(1)}, f32[768]{0:T(1024)}, u32[]{:S(2)}) copy-start(f32[768]{0:T(1024)} %get-tuple-element.74) | copy-start | bytes 9220
  429.1 12.8 %copy-start.7 = (f32[768]{0:T(1024)S(1)}, f32[768]{0:T(1024)}, u32[]{:S(2)}) copy-start(f32[768]{0:T(1024)} %get-tuple-element.75) | copy-start | bytes 9220
  429.1 12.8 %copy-start.8 = (f32[768]{0:T(1024)S(1)}, f32[768]{0:T(1024)}, u32[]{:S(2)}) copy-start(f32[768]{0:T(1024)} %get-tuple-element.76) | copy-start | bytes 9220
  429.1 12.8 %copy-start.9 = (f32[768]{0:T(1024)S(1)}, f32[768]{0:T(1024)}, u32[]{:S(2)}) copy-start(f32[768]{0:T(1024)} %get-tuple-element.77) | copy-start | bytes 9220
  429.1 12.8 %copy-start.10 = (f32[768]{0:T(1024)S(1)}, f32[768]{0:T(1024)}, u32[]{:S(2)}) copy-start(f32[768]{0:T(1024)} %get-tuple-element.78) | copy-start | bytes 9220
  429.1 12.8 %copy-start.11 = (f32[768]{0:T(1024)S(1)}, f32[768]{0:T(1024)}, u32[]{:S(2)}) copy-start(f32[768]{0:T(1024)} %get-tuple-element.79) | copy-start | bytes 9220
  429.1 12.8 %copy-start.12 = (f32[768]{0:T(1024)S(1)}, f32[768]{0:T(1024)}, u32[]{:S(2)}) copy-start(f32[768]{0:T(1024)} %get-tuple-element.80) | copy-start | bytes 9220
  429.2 12.8 %copy-start.13 = (f32[768]{0:T(1024)S(1)}, f32[768]{0:T(1024)}, u32[]{:S(2)}) copy-start(f32[768]{0:T(1024)} %get-tuple-element.81) | copy-start | bytes 9220
  429.2 12.8 %copy-start.14 = (f32[768]{0:T(1024)S(1)}, f32[768]{0:T(1024)}, u32[]{:S(2)}) copy-start(f32[768]{0:T(1024)} %get-tuple-element.82) | copy-start | bytes 9220
  429.2 12.8 %copy-start.15 = (f32[768]{0:T(1024)S(1)}, f32[768]{0:T(1024)}, u32[]{:S(2)}) copy-start(f32[768]{0:T(1024)} %get-tuple-element.83) | copy-start | bytes 9220
  429.2 12.8 %copy-start.16 = (f32[768]{0:T(1024)S(1)}, f32[768]{0:T(1024)}, u32[]{:S(2)}) copy-start(f32[768]{0:T(1024)} %get-tuple-element.84) | copy-start | bytes 9220
  429.2 12.8 %copy-start.17 = (f32[768]{0:T(1024)S(1)}, f32[768]{0:T(1024)}, u32[]{:S(2)}) copy-start(f32[768]{0:T(1024)} %get-tuple-element.85) | copy-start | bytes 9220
  429.2 12.8 %copy-start.18 = (f32[768]{0:T(1024)S(1)}, f32[768]{0:T(1024)}, u32[]{:S(2)}) copy-start(f32[768]{0:T(1024)} %get-tuple-element.86) | copy-start | bytes 9220
  429.2 12.8 %copy-start.19 = (f32[768]{0:T(1024)S(1)}, f32[768]{0:T(1024)}, u32[]{:S(2)}) copy-start(f32[768]{0:T(1024)} %get-tuple-element.87) | copy-start | bytes 9220
  429.2 12.8 %copy-start.20 = (f32[768]{0:T(1024)S(1)}, f32[768]{0:T(1024)}, u32[]{:S(2)}) copy-start(f32[768]{0:T(1024)} %get-tuple-element.88) | copy-start | bytes 9220
  429.2 12.8 %copy-start.21 = (f32[768]{0:T(1024)S(1)}, f32[768]{0:T(1024)}, u32[]{:S(2)}) copy-start(f32[768]{0:T(1024)} %get-tuple-element.89) | copy-start | bytes 9220
  429.2 12.8 %copy-start.22 = (f32[768]{0:T(1024)S(1)}, f32[768]{0:T(1024)}, u32[]{:S(2)}) copy-start(f32[768]{0:T(1024)} %get-tuple-element.90) | copy-start | bytes 9220
  429.3 12.8 %copy-start.23 = (f32[768]{0:T(1024)S(1)}, f32[768]{0:T(1024)}, u32[]{:S(2)}) copy-start(f32[768]{0:T(1024)} %get-tuple-element.91) | copy-start | bytes 9220
  429.3 12.8 %copy-start.24 = (f32[768]{0:T(1024)S(1)}, f32[768]{0:T(1024)}, u32[]{:S(2)}) copy-start(f32[768]{0:T(1024)} %param.21) | copy-start | bytes 9220
  429.3 12.8 %copy-start.25 = (f32[768]{0:T(1024)S(1)}, f32[768]{0:T(1024)}, u32[]{:S(2)}) copy-start(f32[768]{0:T(1024)} %param.20) | copy-start | bytes 9220
  433.3 6.5 %collective-permute-start = (bf16[15,768]{1,0:T(8,128)(2,1)S(1)}, bf16[15,768]{1,0:T(8,128)(2,1)S(1)}, u32[]{:S(2)}, u32[]{:S(2)}) collective-permute-start(bf16[15,768]{1,0:T(8,128)(2,1)S(1)} %get-tuple-element.124), channel_id=1, source_target_pairs={{0,1},{1,2},{2,3},{3,4},{4,5},{5,6},{6,7},{7,8},{8,9},{9,10},{10,1... | collective-permute-start | bytes 69128 | tf_op jit(solution)/shard_map/ppermute | solution.py:17
  436.7 5.1 %collective-permute-start.1 = (bf16[15,768]{1,0:T(8,128)(2,1)S(1)}, bf16[15,768]{1,0:T(8,128)(2,1)S(1)}, u32[]{:S(2)}, u32[]{:S(2)}) collective-permute-start(bf16[15,768]{1,0:T(8,128)(2,1)S(1)} %get-tuple-element.125), channel_id=1, source_target_pairs={{1,0},{2,1},{3,2},{4,3},{5,4},{6,5},{7,6},{8,7},{9,8},{10,9},{11,1... | collective-permute-start | bytes 69128 | tf_op jit(solution)/shard_map/ppermute | solution.py:20
  (59 other events, 255.7 us)
Sparse Core Ops, SparseCore 0:
  9.9 84.2 all-gather.2
  96.0 80.0 all-gather.4
where the time goes:
time: 456 us; the launch traced here: 453 us
  matrix products  160 us (35%)
  waiting for transfers between devices  123 us (27%)
  local copies, waits for them, and re-layouts  113 us (25%)
  other arithmetic  36.8 us (8%)
  between operations  14.5 us (3%)
  starting transfers between devices  5.39 us (1%)
    all_gather x1, waiting for transfers between devices, local(): key_piece = lax.all_gather(keys, 'seq', axis=0, tiled=True)  82.2 us
    dot_general x16, matrix products, attend_block(): jnp.einsum('qhd,khd->hqk', query_heads, key_block, preferred_element_type...  78.1 us
    dot_general x16, matrix products, attend_block(): jnp.einsum('hqk,khd->qhd', weights.astype(jnp.bfloat16), value_block, pre...  75.9 us
    unnamed x51, local copies, waits for them, and re-layouts  57.4 us
    all_gather x1, waiting for transfers between devices, local(): value_piece = lax.all_gather(values, 'seq', axis=0, tiled=True)  37.7 us
    while x144, local copies, waits for them, and re-layouts  19.8 us
    reduce_sum x16, other arithmetic, attend_block(): weight_sum = weight_sum * correction + jnp.sum(weights, axis=2)  16.6 us
    all_gather x1, local copies, waits for them, and re-layouts, local(): key_piece = lax.all_gather(keys, 'seq', axis=0, tiled=True)  16 us
  transfers between devices with their start and end apart: 4, of which 3 were waited for; matrix products, arithmetic and copies ran while one was open for 11% of the time, Pallas kernels for 0%

commit v1 on v0

v1 whole, which is shorter than its diff:
```python
import jax
import jax.numpy as jnp
from jax import lax
from jax.experimental import pallas as pl
from jax.experimental.pallas import tpu as pltpu
from jax.sharding import PartitionSpec as P

MESH = pl.DeviceIdType.MESH
BF16 = jnp.bfloat16
F32 = jnp.float32

HD = 64
TAPS = 31
ROWS = 256
Z = 8
BLOCKS = 12
CHUNK = 1024
EXP_SCALE = 0.125 * 1.4426950408889634

OWN_SLOT = (10, 7, 4, 1, 0, 2, 5, 8)
SHARED_SLOT = (11, 9, 6, 3)
UNROLL = 4


def kernel(
    frames_hbm, q_ref, k_ref, v_ref, wout_hbm, gain_ref, wglu_hbm, dw_ref, bns_ref, bnb_ref,
    att_ref, conv_ref,
    kv_send, q_send, kv, qb, ctx_send, ctx_t, s_scr, mx_scr, m_scr, acc_scr,
    frames, wout, wglu, gpad, taps_tmp, halo_send, halo_recv,
    local_sem, q_ssem, q_rsem, z_ssem, z_rsem, a_ssem, a_rsem, x_ssem, x_rsem, b_ssem, b_rsem,
    c_ssem, c_rsem, h_ssem, h_rsem,
):
    me = lax.axis_index("seq")
    x, z, c = me // 16, lax.rem(me // 2, Z), lax.rem(me, 2)
    odd = lax.rem(z, 2)
    slab = 2 * x + c

    def dev(x, z, c):
        return {"seq": (x * Z + z) * 2 + c}

    def along_z(step):
        return lax.rem(z + step + Z, Z)

    sibling = dev(x, z, 1 - c)
    across = dev(1 - x, z, c)
    left = {"seq": lax.rem(me + 31, 32)}
    right = {"seq": lax.rem(me + 1, 32)}
    other = {"seq": jnp.where(c == 1, lax.rem(me + 1, 32), lax.rem(me + 31, 32))}

    def remote(src, dst, ssem, rsem, to):
        return pltpu.make_async_remote_copy(
            src_ref=src, dst_ref=dst, send_sem=ssem, recv_sem=rsem, device_id=to, device_id_type=MESH
        )

    loads = [
        pltpu.make_async_copy(frames_hbm, frames, local_sem.at[0]),
        pltpu.make_async_copy(wout_hbm, wout, local_sem.at[1]),
        pltpu.make_async_copy(wglu_hbm, wglu, local_sem.at[2]),
    ]
    for load in loads:
        load.start()

    qb[...] = jnp.zeros_like(qb)
    barrier = pltpu.get_barrier_semaphore()
    peers = [dev(x, along_z(d), c) for d in range(1, Z)] + [sibling, across, other]
    for peer in peers:
        pl.semaphore_signal(barrier, inc=1, device_id=peer, device_id_type=MESH)

    q_send[...] = q_ref[...].T.reshape(q_send.shape)
    v_t = v_ref[...].T
    k_all = k_ref[...]
    for zz in range(Z):
        own, shared = 3 * (zz // 2) + 2 * (zz % 2), 3 * (zz // 2) + 1
        kv_send[zz, :ROWS, :] = jnp.concatenate(
            [k_all[:, h * HD : (h + 1) * HD] for h in (own, shared)], axis=1
        )
        v_pair = jnp.concatenate([v_t[h * HD : (h + 1) * HD] for h in (own, shared)], axis=0)
        kv_send[zz, ROWS : ROWS + 128, :] = v_pair[:, :128]
        kv_send[zz, ROWS + 128 :, :] = v_pair[:, 128:]

    def own_head(zz):
        return 3 * (zz // 2) + 2 * lax.rem(zz, 2)

    def shared_head(zz):
        return 3 * (zz // 2) + 1

    def shared_step(i):
        return jnp.where(lax.rem(z + i, 2) == 0, i, -i)

    def home_step(i):
        return jnp.where(odd == 1, i, -i)

    qb[OWN_SLOT[0], :HD, :] = q_send[own_head(z)]
    qb[SHARED_SLOT[0], HD:, :] = q_send[shared_head(z)]
    kv[0, slab] = kv_send[z]

    pl.semaphore_wait(barrier, len(peers))

    def q_own_copy(d):
        to = along_z(d)
        return remote(
            q_send.at[own_head(to)], qb.at[OWN_SLOT[d], pl.ds(0, HD)],
            q_ssem.at[d], q_rsem.at[d], dev(x, to, c),
        )

    def q_shared_copy(i):
        to = along_z(shared_step(i))
        return remote(
            q_send.at[shared_head(to)], qb.at[SHARED_SLOT[i], pl.ds(HD, HD)],
            q_ssem.at[7 + i], q_rsem.at[7 + i], dev(x, to, c),
        )

    def z_copy(d):
        to = along_z(d)
        return remote(kv_send.at[to], kv.at[d, slab], z_ssem.at[d], z_rsem.at[d], dev(x, to, c))

    def sibling_copy(d):
        return remote(kv.at[d, slab], kv.at[d, slab], a_ssem.at[d], a_rsem.at[d], sibling)

    def across_copy(d):
        return remote(kv.at[d, slab], kv.at[d, slab], x_ssem.at[d], x_rsem.at[d], across)

    def second_copy(d):
        there = 2 * (1 - x) + c
        return remote(kv.at[d, there], kv.at[d, there], b_ssem.at[d], b_rsem.at[d], sibling)

    across_copy(0).start()
    sibling_copy(0).start()
    for d in (4, 3, 5, 2, 6, 1, 7):
        q_own_copy(d).start()
        if d <= 3:
            q_shared_copy(d).start()
    for d in (1, 7, 2, 6, 3, 5, 4):
        z_copy(d).start()

    acc_scr[...] = jnp.zeros_like(acc_scr)
    m_scr[...] = jnp.full_like(m_scr, -1e30)
    ones = jnp.ones((16, CHUNK), BF16)

    def chunk_at(t):
        return lax.rem(jnp.where(lax.rem(t, 2) == 1, (t + 1) // 2, Z - t // 2), Z)

    def first_hop(t):
        d = chunk_at(t)
        z_copy(d).wait_recv()
        across_copy(d).start()
        sibling_copy(d).start()

    def second_hop(t):
        d = chunk_at(t)
        across_copy(d).wait_recv()
        second_copy(d).start()

    def arrived(t):
        d = chunk_at(t)
        sibling_copy(d).wait_recv()
        second_copy(d).wait_recv()

    def scores(t, b, slot):
        d = chunk_at(t)
        query = qb[b]
        top = None
        for s in range(4):
            part = jnp.dot(kv[d, s, :ROWS, :], query, preferred_element_type=F32)
            s_scr[slot, s * ROWS : (s + 1) * ROWS, :] = part
            part_top = jnp.max(part.reshape(ROWS // 8, 8, ROWS), axis=0)
            top = part_top if top is None else jnp.maximum(top, part_top)
        mx_scr[slot] = jnp.max(top, axis=0, keepdims=True) * EXP_SCALE

    def weigh(t, b, slot):
        d = chunk_at(t)
        is_shared = (b == SHARED_SLOT[0]) | (b == SHARED_SLOT[1]) | (b == SHARED_SLOT[2]) | (b == SHARED_SLOT[3])
        head_row = pl.multiple_of(jnp.where(is_shared, HD, 0), HD)
        old = m_scr[b]
        new = jnp.maximum(old, mx_scr[slot])
        m_scr[b] = new
        weights, values = [], []
        for s in range(4):
            part = s_scr[slot, s * ROWS : (s + 1) * ROWS, :] * EXP_SCALE - new
            weights.append(jnp.exp2(part).astype(BF16))
            values.append(kv[d, s, pl.ds(ROWS + head_row, HD), :])
            values.append(kv[d, s, pl.ds(ROWS + 128 + head_row, HD), :])
        values = jnp.concatenate([jnp.concatenate(values, axis=1), ones], axis=0)
        product = jnp.dot(values, jnp.concatenate(weights, axis=0), preferred_element_type=F32)
        total = acc_scr[b] * jnp.exp2(old - new) + product
        acc_scr[b] = total
        return total

    second_hop(0)
    first_hop(1)
    for d in range(1, Z):
        q_own_copy(d).wait_recv()
    for i in range(1, 4):
        q_shared_copy(i).wait_recv()
    arrived(0)
    scores(0, 0, 0)

    groups = BLOCKS // UNROLL

    def step(i, carry):
        t, g = i // groups, lax.rem(i, groups)

        @pl.when((g == 0) & (t < Z - 2))
        def _():
            first_hop(t + 2)

        @pl.when(g == 1)
        def _():
            second_hop(t + 1)

        @pl.when(g == 2)
        def _():
            arrived(t + 1)

        for u in range(UNROLL):
            n = i * UNROLL + u
            scores((n + 1) // BLOCKS, lax.rem(n + 1, BLOCKS), (u + 1) % 2)
            weigh(n // BLOCKS, lax.rem(n, BLOCKS), u % 2)
        return carry

    lax.fori_loop(0, (Z - 1) * groups, step, 0)

    def context_copy(b):
        if b in OWN_SLOT:
            d = OWN_SLOT.index(b)
            to, head, sem = along_z(-d), own_head(z), d
        else:
            i = SHARED_SLOT.index(b)
            to, head, sem = along_z(home_step(i)), shared_head(z), 7 + i
        return remote(ctx_send.at[b], ctx_t.at[head], c_ssem.at[sem], c_rsem.at[sem], dev(x, to, c))

    home_slots = (OWN_SLOT[0], SHARED_SLOT[0])
    for b in range(BLOCKS):
        if b + 1 < BLOCKS:
            scores(Z - 1, b + 1, (b + 1) % 2)
        total = weigh(Z - 1, b, b % 2)
        context = (total[:HD] / total[HD : HD + 1]).astype(BF16)
        if b == OWN_SLOT[0]:
            ctx_t[own_head(z)] = context
        elif b == SHARED_SLOT[0]:
            ctx_t[shared_head(z)] = context
        else:
            ctx_send[b] = context
            context_copy(b).start()

    for load in loads:
        load.wait()
    for b in range(BLOCKS):
        if b not in home_slots:
            context_copy(b).wait_recv()

    context = ctx_t[...].reshape(BLOCKS * HD, ROWS).T
    residual = frames[...].astype(F32) + jnp.dot(context, wout[...], preferred_element_type=F32)
    att_ref[...] = residual.astype(BF16)
    centered = residual - jnp.mean(residual, axis=1, keepdims=True)
    variance = jnp.mean(centered * centered, axis=1, keepdims=True)
    normed = (centered * lax.rsqrt(variance + 1e-05) * gain_ref[...]).astype(BF16)
    projected = jnp.dot(normed, wglu[...], preferred_element_type=F32)
    channels = projected.shape[1] // 2
    gated = (projected[:, :channels] * jax.nn.sigmoid(projected[:, channels:])).astype(BF16)

    halo_send[0] = gated[:16]
    halo_send[1] = gated[ROWS - 16 :]
    to_left = remote(halo_send.at[0], halo_recv.at[1], h_ssem.at[0], h_rsem.at[1], left)
    to_right = remote(halo_send.at[1], halo_recv.at[0], h_ssem.at[1], h_rsem.at[0], right)
    to_left.start()
    to_right.start()
    gpad[16 : 16 + ROWS, :] = gated.astype(F32)
    to_left.wait_recv()
    to_right.wait_recv()
    gpad[:16, :] = jnp.where(me == 0, 0.0, halo_recv[0].astype(F32))
    gpad[16 + ROWS :, :] = jnp.where(me == 31, 0.0, halo_recv[1].astype(F32))

    for col in range(0, channels, 128):
        cols = slice(col, col + 128)
        conv = None
        for r in range(8):
            part = None
            for u in range(r, 32, 8):
                if u == 0:
                    continue
                term = gpad[u - r : u - r + ROWS + 8, cols] * dw_ref[u - 1 : u, cols]
                part = term if part is None else part + term
            taps_tmp[r] = part
            shifted = taps_tmp[r, r : r + ROWS, :]
            conv = shifted if conv is None else conv + shifted
        u = bns_ref[:, cols] * conv + bnb_ref[:, cols]
        conv_ref[:, cols] = (u * jax.nn.sigmoid(u)).astype(BF16)

    for d in range(Z):
        if d:
            q_own_copy(d).wait_send()
            z_copy(d).wait_send()
        across_copy(d).wait_send()
        sibling_copy(d).wait_send()
        second_copy(d).wait_send()
    for i in range(1, 4):
        q_shared_copy(i).wait_send()
    for b in range(BLOCKS):
        if b not in home_slots:
            context_copy(b).wait_send()
    to_left.wait_send()
    to_right.wait_send()


def local(frames_in, queries, keys, values, w_out, ln_gain, w_glu, dw_weight, bn_scale, bn_shift):
    rows, width = frames_in.shape
    channels = w_glu.shape[1] // 2
    vmem, hbm = pl.BlockSpec(memory_space=pltpu.VMEM), pl.BlockSpec(memory_space=pl.ANY)
    sems = [pltpu.SemaphoreType.DMA((n,)) for n in (3, 11, 11, Z, Z, Z, Z, Z, Z, Z, Z, 11, 11, 2, 2)]
    return pl.pallas_call(
        kernel,
        out_shape=(
            jax.ShapeDtypeStruct((rows, width), BF16),
            jax.ShapeDtypeStruct((rows, channels), BF16),
        ),
        in_specs=[hbm, vmem, vmem, vmem, hbm, vmem, hbm, vmem, vmem, vmem],
        out_specs=(vmem, vmem),
        scratch_shapes=[
            pltpu.VMEM((Z, 2 * ROWS, 128), BF16),
            pltpu.VMEM((BLOCKS, HD, ROWS), BF16),
            pltpu.VMEM((Z, 4, 2 * ROWS, 128), BF16),
            pltpu.VMEM((BLOCKS, 2 * HD, ROWS), BF16),
            pltpu.VMEM((BLOCKS, HD, ROWS), BF16),
            pltpu.VMEM((BLOCKS, HD, ROWS), BF16),
            pltpu.VMEM((2, CHUNK, ROWS), F32),
            pltpu.VMEM((2, 1, ROWS), F32),
            pltpu.VMEM((BLOCKS, 1, ROWS), F32),
            pltpu.VMEM((BLOCKS, HD + 16, ROWS), F32),
            pltpu.VMEM((rows, width), BF16),
            pltpu.VMEM(w_out.shape, BF16),
            pltpu.VMEM(w_glu.shape, BF16),
            pltpu.VMEM((ROWS + 32, channels), F32),
            pltpu.VMEM((8, ROWS + 8, 128), F32),
            pltpu.VMEM((2, 16, channels), BF16),
            pltpu.VMEM((2, 16, channels), BF16),
        ]
        + sems,
        compiler_params=pltpu.CompilerParams(
            collective_id=0, has_side_effects=True, vmem_limit_bytes=56 * 2**20
        ),
    )(
        frames_in, queries, keys, values, w_out, ln_gain.reshape(1, -1), w_glu, dw_weight,
        bn_scale.reshape(1, -1), bn_shift.reshape(1, -1),
    )


def solution(mesh):
    split = P(("dp", "seq"), None)
    return jax.shard_map(
        local,
        mesh=mesh,
        in_specs=(split,) * 4 + (P(),) * 6,
        out_specs=(split, split),
        check_vma=False,
    )
```

time: 456 us -> 85.2 us (0.19)
  matrix products: 160 us -> 0 us
  waiting for transfers between devices: 123 us -> 0 us
  local copies, waits for them, and re-layouts: 113 us -> 7.65 us
  Pallas kernels: 0 us -> 76.7 us
  other arithmetic: 36.8 us -> 0 us
  between operations: 14.5 us -> 0.64 us
  starting transfers between devices: 5.39 us -> 0 us
    dot_general x34 -> x0, matrix products: 160 us -> none  [the longest x16 78.1 us: attend_block(): jnp.einsum('qhd,khd->hqk', query_heads, key_block, preferred_element_type...]
    all_gather x2 -> x0, waiting for transfers between devices: 120 us -> none  [the longest x1 82.2 us: local(): key_piece = lax.all_gather(keys, 'seq', axis=0, tiled=True)]
    pallas_call x0 -> x1, Pallas kernels: none -> 76.7 us  [local(): pl.pallas_call(kernel, out_shape=(jax.ShapeDtypeStruct((rows, width), BF1...]
    unnamed x51 -> x2, local copies, waits for them, and re-layouts: 57.4 us -> 3.83 us
    all_gather x2 -> x0, local copies, waits for them, and re-layouts: 32 us -> none  [the longest x1 16 us: local(): key_piece = lax.all_gather(keys, 'seq', axis=0, tiled=True)]
    while x144 -> x0, local copies, waits for them, and re-layouts: 19.8 us -> none
    reduce_sum x17 -> x0, other arithmetic: 17.8 us -> none  [the longest x16 16.6 us: attend_block(): weight_sum = weight_sum * correction + jnp.sum(weights, axis=2)]
    transpose x16 -> x0, other arithmetic: 13.2 us -> none  [attend_block(): accumulated = accumulated * correction.T[:, :, None] + product]
  transfers between devices with their start and end apart: 4 -> 0, of which waited for: 3 -> 0; matrix products, arithmetic and copies ran while one was open for 11% -> 0% of each run, Pallas kernels for 0% -> 0%
where the time goes in v1:
time: 85.2 us; the launch traced here: 85 us
  Pallas kernels  76.7 us (90%)
  local copies, waits for them, and re-layouts  7.65 us (9%)
    pallas_call x1, Pallas kernels, local(): pl.pallas_call(kernel, out_shape=(jax.ShapeDtypeStruct((rows, width), BF1...  76.7 us
    unnamed x2, local copies, waits for them, and re-layouts  3.83 us

profile of v1, /device:TPU:1, one launch (start us, length us, event | category | flops | bytes accessed | tf_op | source)
XLA Modules:
  0.0 85.0 jit_solution(17612338166918063192)
XLA Ops:
  0.6 1.3 %reshape.14.bns_ref = f32[1,768]{1,0:T(1,128)} reshape(f32[768]{0:T(1024)} %param.18) | data formatting | bytes 6144 | tf_op jit(solution)/shard_map/reshape | solution.py:344
  1.9 1.3 %reshape.15.bnb_ref = f32[1,768]{1,0:T(1,128)} reshape(f32[768]{0:T(1024)} %param.19) | data formatting | bytes 6144 | tf_op jit(solution)/shard_map/reshape | solution.py:344
  3.2 1.3 %reshape.13.gain_ref = f32[1,1536]{1,0:T(1,128)} reshape(f32[1536]{0:T(1024)} %param.15) | data formatting | bytes 12288 | tf_op jit(solution)/shard_map/reshape | solution.py:343
  4.5 76.7 %shard_map.113 = (bf16[256,1536]{1,0:T(8,128)(2,1)}, bf16[256,768]{1,0:T(8,128)(2,1)}) custom-call(bf16[256,1536]{1,0:T(8,128)(2,1)} %frames_hbm.1, bf16[256,768]{1,0:T(8,128)(2,1)} %q_ref.1, bf16[256,768]{1,0:T(8,128)(2,1)} %k_ref.1, bf16[256,768]{1,0:T(8,128)(2,1)} %v_ref.1, bf16[768,1536]{1,0:T(8,128)(2,1)} %wout_hbm.1, f32[1,1536]{1,0:T(1,128)} %reshape.13.gain_ref, ...), custom_call_target="tpu_custom_call" | custom-call | tf_op jit(solution)/shard_map/pallas_call | solution.py:311
  81.1 2.1 %copy.14 = bf16[256,1536]{1,0:T(8,128)(2,1)} copy(bf16[256,1536]{1,0:T(8,128)(2,1)} %get-tuple-element.4) | data formatting | bytes 1572864
  83.2 1.8 %copy.15 = bf16[256,768]{1,0:T(8,128)(2,1)} copy(bf16[256,768]{1,0:T(8,128)(2,1)} %get-tuple-element.5) | data formatting | bytes 786432

commit v2 on v1

v2 whole, which is shorter than its diff:
```python
import jax
import jax.numpy as jnp
from jax import lax
from jax.experimental import pallas as pl
from jax.experimental.pallas import tpu as pltpu
from jax.sharding import PartitionSpec as P

MESH = pl.DeviceIdType.MESH
BF16 = jnp.bfloat16
F32 = jnp.float32

HD = 64
TAPS = 31
ROWS = 256
Z = 8
HALF = ROWS // 2
CHUNK = 1024
EXP_SCALE = 0.125 * 1.4426950408889634
OWN_HEADS = (0, 2, 3, 5, 6, 8, 9, 11)
SHARED_HEADS = (1, 4, 7, 10)
EDGE = 16

STEPS = (0, 1, 7, 2, 6, 3, 5, 4)
OWN, SHARED = 0, 1


def kernel(
    frames_hbm, q_ref, k_ref, v_ref, wout_hbm, gain_ref, wglu_hbm, dw_ref, bns_ref, bnb_ref,
    att_ref, conv_ref,
    kv_send, q_send, kv, qb, ctx_send, ctx_t, s_scr, mx_scr, m_scr, acc_scr,
    frames, wout, wglu, gpad, taps_tmp, halo_send, halo_recv,
    local_sem, q_ssem, q_rsem, z_ssem, z_rsem, a_ssem, a_rsem, x_ssem, x_rsem, b_ssem, b_rsem,
    p_ssem, p_rsem, c_ssem, c_rsem, h_ssem, h_rsem,
):
    me = lax.axis_index("seq")
    x, z, c = me // 16, lax.rem(me // 2, Z), lax.rem(me, 2)
    odd = lax.rem(z, 2)
    slab, slab_across = 2 * x + c, 2 * (1 - x) + c

    def dev(x, z, c):
        return {"seq": (x * Z + z) * 2 + c}

    def along_z(step):
        return lax.rem(z + step + Z, Z)

    sibling = dev(x, z, 1 - c)
    across = dev(1 - x, z, c)
    partner = dev(x, z + 1 - 2 * odd, c)
    left = {"seq": lax.rem(me + 31, 32)}
    right = {"seq": lax.rem(me + 1, 32)}
    other = {"seq": jnp.where(c == 1, lax.rem(me + 1, 32), lax.rem(me + 31, 32))}

    def remote(src, dst, ssem, rsem, to):
        return pltpu.make_async_remote_copy(
            src_ref=src, dst_ref=dst, send_sem=ssem, recv_sem=rsem, device_id=to, device_id_type=MESH
        )

    barrier = pltpu.get_barrier_semaphore()
    peers = [dev(x, along_z(d), c) for d in range(1, Z)] + [sibling, across, other]
    for peer in peers:
        pl.semaphore_signal(barrier, inc=1, device_id=peer, device_id_type=MESH)

    loads = [
        pltpu.make_async_copy(frames_hbm, frames, local_sem.at[0]),
        pltpu.make_async_copy(wout_hbm, wout, local_sem.at[1]),
        pltpu.make_async_copy(wglu_hbm, wglu, local_sem.at[2]),
    ]
    for load in loads:
        load.start()

    q_send[...] = q_ref[...].T.reshape(q_send.shape)
    v_t = v_ref[...].T
    for head in range(12):
        cols = slice(head * HD, (head + 1) * HD)
        kv_send[head, :HALF, :] = jnp.concatenate([k_ref[:HALF, cols], k_ref[HALF:, cols]], axis=1)
        kv_send[head, HALF : HALF + HD, :] = v_t[cols, :HALF]
        kv_send[head, HALF + HD :, :] = v_t[cols, HALF:]

    def own_head(zz):
        return 3 * (zz // 2) + 2 * lax.rem(zz, 2)

    def shared_head(zz):
        return 3 * (zz // 2) + 1

    def shared_step(i):
        return jnp.where(lax.rem(z + i, 2) == 0, i, -i)

    def home_step(i):
        return jnp.where(odd == 1, i, -i)

    qb[0] = q_send[own_head(z)]
    qb[8] = q_send[shared_head(z)]
    kv[OWN, 0, slab] = kv_send[own_head(z)]
    kv[SHARED, 0, slab] = kv_send[shared_head(z)]

    pl.semaphore_wait(barrier, len(peers))

    def q_own_copy(n):
        to = along_z(STEPS[n])
        return remote(q_send.at[own_head(to)], qb.at[n], q_ssem.at[n], q_rsem.at[n], dev(x, to, c))

    def q_shared_copy(i):
        to = along_z(shared_step(i))
        return remote(
            q_send.at[shared_head(to)], qb.at[8 + i], q_ssem.at[8 + i], q_rsem.at[8 + i], dev(x, to, c)
        )

    def own_z_copy(n, step):
        to = along_z(step)
        return remote(
            kv_send.at[own_head(to)], kv.at[OWN, n, slab], z_ssem.at[OWN, n], z_rsem.at[OWN, n], dev(x, to, c)
        )

    def shared_z_copy(i):
        to = along_z(shared_step(i))
        return remote(
            kv_send.at[shared_head(to)], kv.at[SHARED, 2 * i, slab],
            z_ssem.at[SHARED, i], z_rsem.at[SHARED, i], dev(x, to, c),
        )

    def partner_copy(i):
        return remote(
            kv.at[SHARED, 2 * i, slab], kv.at[SHARED, 2 * i + 1, slab], p_ssem.at[i], p_rsem.at[i], partner
        )

    def sibling_copy(h, n):
        part = kv.at[h, n, slab]
        return remote(part, part, a_ssem.at[h, n], a_rsem.at[h, n], sibling)

    def across_copy(h, n):
        part = kv.at[h, n, slab]
        return remote(part, part, x_ssem.at[h, n], x_rsem.at[h, n], across)

    def second_copy(h, n):
        part = kv.at[h, n, slab_across]
        return remote(part, part, b_ssem.at[h, n], b_rsem.at[h, n], sibling)

    def spread(h, n):
        across_copy(h, n).start()
        sibling_copy(h, n).start()

    def own_first(n):
        own_z_copy(n, 0).wait_recv()
        spread(OWN, n)

    def shared_first(n):
        if n % 2 == 0:
            shared_z_copy(n // 2).wait_recv()
            partner_copy(n // 2).start()
        else:
            partner_copy(n // 2).wait_recv()
        spread(SHARED, n)

    def second(h, n):
        across_copy(h, n).wait_recv()
        second_copy(h, n).start()

    def arrived(h, n):
        sibling_copy(h, n).wait_recv()
        second_copy(h, n).wait_recv()

    spread(OWN, 0)
    for n in (1, 2):
        own_z_copy(n, STEPS[n]).start()
    for n in range(1, Z):
        q_own_copy(n).start()
    spread(SHARED, 0)
    partner_copy(0).start()
    for i in range(1, 4):
        q_shared_copy(i).start()
    for n in range(3, Z):
        own_z_copy(n, STEPS[n]).start()
    for i in range(1, 4):
        shared_z_copy(i).start()

    acc_scr[...] = jnp.zeros_like(acc_scr)
    m_scr[...] = jnp.full_like(m_scr, -1e30)
    ones = jnp.ones((16, CHUNK), BF16)
    zeros = jnp.zeros((HD, ROWS), BF16)

    def scores(h, n, b, slot):
        query = qb[b]
        keys = jnp.concatenate([kv[h, n, s, :HALF, :] for s in range(4)], axis=0)
        top = None
        for half in range(2):
            weight = jnp.concatenate([query, zeros] if half == 0 else [zeros, query], axis=0)
            part = jnp.dot(keys, weight, preferred_element_type=F32)
            s_scr[slot, half * 4 * HALF : (half + 1) * 4 * HALF, :] = part
            part_top = jnp.max(part.reshape(HALF // 2, 8, ROWS), axis=0)
            top = part_top if top is None else jnp.maximum(top, part_top)
        mx_scr[slot] = jnp.max(top, axis=0, keepdims=True) * EXP_SCALE

    def weigh(h, n, b, slot):
        old = m_scr[b]
        new = jnp.maximum(old, mx_scr[slot])
        m_scr[b] = new
        weights, values = [], []
        for half in range(2):
            part = s_scr[slot, half * 4 * HALF : (half + 1) * 4 * HALF, :] * EXP_SCALE - new
            weights.append(jnp.exp2(part).astype(BF16))
            first = HALF + half * HD
            values += [kv[h, n, s, first : first + HD, :] for s in range(4)]
        values = jnp.concatenate([jnp.concatenate(values, axis=1), ones], axis=0)
        product = jnp.dot(values, jnp.concatenate(weights, axis=0), preferred_element_type=F32)
        total = acc_scr[b] * jnp.exp2(old - new) + product
        acc_scr[b] = total
        return total

    def context_copy(b):
        if b < 8:
            to, head = along_z(-STEPS[b]), own_head(z)
        else:
            to, head = along_z(home_step(b - 8)), shared_head(z)
        return remote(ctx_send.at[b], ctx_t.at[head], c_ssem.at[b], c_rsem.at[b], dev(x, to, c))

    def finish(b, total):
        context = (total[:HD] / total[HD : HD + 1]).astype(BF16)
        if b == 0:
            ctx_t[own_head(z)] = context
        elif b == 8:
            ctx_t[shared_head(z)] = context
        else:
            ctx_send[b] = context
            context_copy(b).start()

    def place(r, u):
        if isinstance(r, int):
            if r == 3 or r > 8:
                return SHARED, 2 * (0 if r == 3 else r - 8) + u // 4, 8 + u % 4
            return OWN, r - (r > 3), u
        is_shared = (r == 3) | (r > 8)
        unit = jnp.where(is_shared, 2 * jnp.where(r == 3, 0, r - 8) + u // 4, r - jnp.where(r > 3, 1, 0))
        return jnp.where(is_shared, SHARED, OWN), unit, jnp.where(is_shared, 8 + u % 4, u)

    plan = {
        (1, 4): lambda: second(SHARED, 1),
        (1, 7): lambda: arrived(OWN, 2),
        (2, 0): lambda: own_first(3),
        (2, 4): lambda: own_first(4),
        (2, 7): lambda: (arrived(SHARED, 0), arrived(SHARED, 1), [q_shared_copy(i).wait_recv() for i in (1, 2, 3)]),
        (3, 0): lambda: second(OWN, 3),
        (3, 4): lambda: second(OWN, 4),
        (3, 7): lambda: arrived(OWN, 3),
        (4, 0): lambda: own_first(5),
        (4, 4): lambda: own_first(6),
        (4, 7): lambda: arrived(OWN, 4),
        (5, 0): lambda: second(OWN, 5),
        (5, 4): lambda: (second(OWN, 6), own_first(7)),
        (5, 7): lambda: arrived(OWN, 5),
        (6, 0): lambda: shared_first(2),
        (6, 4): lambda: second(OWN, 7),
        (6, 7): lambda: arrived(OWN, 6),
        (7, 0): lambda: shared_first(4),
        (7, 4): lambda: (shared_first(6), second(SHARED, 2)),
        (7, 7): lambda: arrived(OWN, 7),
        (9, 0): lambda: second(SHARED, 5),
        (9, 4): lambda: second(SHARED, 7),
        (9, 7): lambda: (arrived(SHARED, 4), arrived(SHARED, 5)),
        (10, 7): lambda: (arrived(SHARED, 6), arrived(SHARED, 7)),
    }

    def pass_on(r, u):
        for (at, step), action in plan.items():
            if step == u:
                pl.when(r == at)(lambda action=action: (action(), None)[1])

    def round_of_eight(r, carry):
        for u in range(8):
            pass_on(r, u)
            scores(*(place(r, u + 1) if u < 7 else place(r + 1, 0)), (u + 1) % 2)
            weigh(*place(r, u), u % 2)
        return carry

    second(OWN, 0)
    arrived(OWN, 0)
    scores(OWN, 0, 0, 0)
    for u in range(8):
        if u == 2:
            own_first(1)
            own_first(2)
        if u == 4:
            second(SHARED, 0)
            shared_first(1)
        if u == 6:
            second(OWN, 1)
            second(OWN, 2)
        if u < 7:
            q_own_copy(u + 1).wait_recv()
            scores(OWN, 0, u + 1, (u + 1) % 2)
        else:
            arrived(OWN, 1)
            scores(OWN, 1, 0, 0)
        weigh(OWN, 0, u, u % 2)

    lax.fori_loop(1, 8, round_of_eight, 0)

    order = (0, 7, 6, 5, 4, 3, 2, 1)
    for u, b in enumerate(order):
        if u == 0:
            shared_first(3)
        if u == 2:
            second(SHARED, 4)
        if u == 4:
            shared_first(5)
            second(SHARED, 6)
        if u == 6:
            shared_first(7)
            second(SHARED, 3)
        if u < 7:
            scores(OWN, 7, order[u + 1], (u + 1) % 2)
        else:
            arrived(SHARED, 2)
            arrived(SHARED, 3)
            scores(SHARED, 2, 8, 0)
        finish(b, weigh(OWN, 7, b, u % 2))

    lax.fori_loop(9, 11, round_of_eight, 0)

    for u in range(8):
        if u < 7:
            scores(*place(11, u + 1), (u + 1) % 2)
        total = weigh(*place(11, u), u % 2)
        if u >= 4:
            finish(4 + u, total)

    for load in loads:
        load.wait()

    def project(heads):
        context = jnp.concatenate([ctx_t[h] for h in heads], axis=0).T
        weight = jnp.concatenate([wout[h * HD : (h + 1) * HD, :] for h in heads], axis=0)
        return jnp.dot(context, weight, preferred_element_type=F32)

    for b in range(1, 8):
        context_copy(b).wait_recv()
    residual = frames[...].astype(F32) + project(OWN_HEADS)
    for b in range(9, 12):
        context_copy(b).wait_recv()
    residual = residual + project(SHARED_HEADS)
    att_ref[...] = residual.astype(BF16)
    centered = residual - jnp.mean(residual, axis=1, keepdims=True)
    variance = jnp.mean(centered * centered, axis=1, keepdims=True)
    gain = gain_ref[...].reshape(1, -1)
    normed = (centered * lax.rsqrt(variance + 1e-05) * gain).astype(BF16)
    projected = jnp.dot(normed, wglu[...], preferred_element_type=F32)
    channels = projected.shape[1] // 2
    gated = (projected[:, :channels] * jax.nn.sigmoid(projected[:, channels:])).astype(BF16)

    halo_send[0] = gated[:EDGE]
    halo_send[1] = gated[ROWS - EDGE :]
    to_left = remote(halo_send.at[0], halo_recv.at[1], h_ssem.at[0], h_rsem.at[1], left)
    to_right = remote(halo_send.at[1], halo_recv.at[0], h_ssem.at[1], h_rsem.at[0], right)
    to_left.start()
    to_right.start()
    gpad[EDGE : EDGE + ROWS, :] = gated.astype(F32)
    bn_scale, bn_shift = bns_ref[...].reshape(1, -1), bnb_ref[...].reshape(1, -1)

    def convolve(first, rows):
        for col in range(0, channels, 128):
            cols = slice(col, col + 128)
            conv = None
            for r in range(8):
                part = None
                for u in range(r, 32, 8):
                    if u == 0:
                        continue
                    begin = first + u - r
                    term = gpad[begin : begin + rows + 8, cols] * dw_ref[u - 1 : u, cols]
                    part = term if part is None else part + term
                taps_tmp[r, : rows + 8] = part
                shifted = taps_tmp[r, r : r + rows, :]
                conv = shifted if conv is None else conv + shifted
            u = bn_scale[:, cols] * conv + bn_shift[:, cols]
            conv_ref[first : first + rows, cols] = (u * jax.nn.sigmoid(u)).astype(BF16)

    convolve(EDGE, ROWS - 2 * EDGE)
    to_left.wait_recv()
    to_right.wait_recv()
    gpad[:EDGE, :] = jnp.where(me == 0, 0.0, halo_recv[0].astype(F32))
    gpad[EDGE + ROWS :, :] = jnp.where(me == 31, 0.0, halo_recv[1].astype(F32))
    convolve(0, EDGE)
    convolve(ROWS - EDGE, EDGE)

    for n in range(1, Z):
        q_own_copy(n).wait_send()
        own_z_copy(n, STEPS[n]).wait_send()
    for i in range(1, 4):
        q_shared_copy(i).wait_send()
        shared_z_copy(i).wait_send()
    for i in range(4):
        partner_copy(i).wait_send()
    for h in (OWN, SHARED):
        for n in range(Z):
            across_copy(h, n).wait_send()
            sibling_copy(h, n).wait_send()
            second_copy(h, n).wait_send()
    for b in range(12):
        if b not in (0, 8):
            context_copy(b).wait_send()
    to_left.wait_send()
    to_right.wait_send()


def hand_on(att_in, conv_in, att_out, conv_out):
    att_out[...] = att_in[...]
    conv_out[...] = conv_in[...]


def local(frames_in, queries, keys, values, w_out, ln_gain, w_glu, dw_weight, bn_scale, bn_shift):
    rows, width = frames_in.shape
    channels = w_glu.shape[1] // 2
    vmem, hbm = pl.BlockSpec(memory_space=pltpu.VMEM), pl.BlockSpec(memory_space=pl.ANY)
    dma = pltpu.SemaphoreType.DMA
    units = [dma((2, Z))] * 8
    out_shape = (
        jax.ShapeDtypeStruct((rows, width), BF16),
        jax.ShapeDtypeStruct((rows, channels), BF16),
    )
    results = pl.pallas_call(
        kernel,
        out_shape=out_shape,
        in_specs=[hbm, vmem, vmem, vmem, hbm, vmem, hbm, vmem, vmem, vmem],
        out_specs=(vmem, vmem),
        scratch_shapes=[
            pltpu.VMEM((12, ROWS, 128), BF16),
            pltpu.VMEM((12, HD, ROWS), BF16),
            pltpu.VMEM((2, Z, 4, ROWS, 128), BF16),
            pltpu.VMEM((12, HD, ROWS), BF16),
            pltpu.VMEM((12, HD, ROWS), BF16),
            pltpu.VMEM((12, HD, ROWS), BF16),
            pltpu.VMEM((2, CHUNK, ROWS), F32),
            pltpu.VMEM((2, 1, ROWS), F32),
            pltpu.VMEM((12, 1, ROWS), F32),
            pltpu.VMEM((12, HD + 16, ROWS), F32),
            pltpu.VMEM((rows, width), BF16),
            pltpu.VMEM(w_out.shape, BF16),
            pltpu.VMEM(w_glu.shape, BF16),
            pltpu.VMEM((ROWS + 2 * EDGE, channels), F32),
            pltpu.VMEM((8, ROWS + 8, 128), F32),
            pltpu.VMEM((2, EDGE, channels), BF16),
            pltpu.VMEM((2, EDGE, channels), BF16),
            dma((3,)),
            dma((12,)),
            dma((12,)),
        ]
        + units
        + [dma((4,)), dma((4,)), dma((12,)), dma((12,)), dma((2,)), dma((2,))],
        compiler_params=pltpu.CompilerParams(
            collective_id=0, has_side_effects=True, vmem_limit_bytes=56 * 2**20
        ),
    )(frames_in, queries, keys, values, w_out, ln_gain, w_glu, dw_weight, bn_scale, bn_shift)
    return pl.pallas_call(
        hand_on,
        out_shape=out_shape,
        in_specs=[vmem, vmem],
        out_specs=(vmem, vmem),
    )(*results)


def solution(mesh):
    split = P(("dp", "seq"), None)
    return jax.shard_map(
        local,
        mesh=mesh,
        in_specs=(split,) * 4 + (P(),) * 6,
        out_specs=(split, split),
        check_vma=False,
    )
```

time: 85.2 us -> 78.1 us (0.917)
  local copies, waits for them, and re-layouts: 7.65 us -> 0 us
    unnamed x2 -> x0, local copies, waits for them, and re-layouts: 3.83 us -> none
    reshape x3 -> x0, local copies, waits for them, and re-layouts: 3.82 us -> none  [the longest x1 1.29 us: local(): ln_gain.reshape(1, -1)]
    pallas_call x1 -> x2, Pallas kernels: 76.7 us -> 77.3 us  [the longest x1 75 us: local(): pl.pallas_call(kernel, out_shape=out_shape, in_specs=[hbm, vmem, vmem, vm...]
where the time goes in v2:
time: 78.1 us; the launch traced here: 78 us
  Pallas kernels  77.3 us (99%)
    pallas_call x1, Pallas kernels, local(): pl.pallas_call(kernel, out_shape=out_shape, in_specs=[hbm, vmem, vmem, vm...  75 us
    pallas_call x1, Pallas kernels, local(): pl.pallas_call(hand_on, out_shape=out_shape, in_specs=[vmem, vmem], out_s...  2.29 us

profile of v2, /device:TPU:1, one launch (start us, length us, event | category | flops | bytes accessed | tf_op | source)
XLA Modules:
  0.0 78.0 jit_solution(9443111369277602793)
XLA Ops:
  0.6 75.0 %shard_map.113 = (bf16[256,1536]{1,0:T(8,128)(2,1)}, bf16[256,768]{1,0:T(8,128)(2,1)}) custom-call(bf16[256,1536]{1,0:T(8,128)(2,1)} %frames_hbm.1, bf16[256,768]{1,0:T(8,128)(2,1)} %q_ref.1, bf16[256,768]{1,0:T(8,128)(2,1)} %k_ref.1, bf16[256,768]{1,0:T(8,128)(2,1)} %v_ref.1, bf16[768,1536]{1,0:T(8,128)(2,1)} %wout_hbm.1, f32[1536]{0:T(1024)} %gain_ref.1, ...), custom_call_target="tpu_custom_call" | custom-call | tf_op jit(solution)/shard_map/pallas_call | solution.py:419
  75.7 2.3 %shard_map.114 = (bf16[256,1536]{1,0:T(8,128)(2,1)}, bf16[256,768]{1,0:T(8,128)(2,1)}) custom-call(bf16[256,1536]{1,0:T(8,128)(2,1)} %get-tuple-element.4.att_in, bf16[256,768]{1,0:T(8,128)(2,1)} %get-tuple-element.5.conv_in), custom_call_target="tpu_custom_call" | custom-call | tf_op jit(solution)/shard_map/pallas_call | solution.py:452

commit v3 on v2

--- a/solution.py
+++ b/solution.py
@@ -166,12 +166,12 @@
         q_own_copy(n).start()
     spread(SHARED, 0)
     partner_copy(0).start()
+    for n in (3, 4):
+        own_z_copy(n, STEPS[n]).start()
     for i in range(1, 4):
         q_shared_copy(i).start()
-    for n in range(3, Z):
+    for n in (5, 6, 7):
         own_z_copy(n, STEPS[n]).start()
-    for i in range(1, 4):
-        shared_z_copy(i).start()
 
     acc_scr[...] = jnp.zeros_like(acc_scr)
     m_scr[...] = jnp.full_like(m_scr, -1e30)
@@ -223,105 +223,84 @@
             ctx_send[b] = context
             context_copy(b).start()
 
+    shared_units = {3: (0, 1), 9: (2, 4), 10: (6, 3), 11: (5, 7)}
+
     def place(r, u):
         if isinstance(r, int):
-            if r == 3 or r > 8:
-                return SHARED, 2 * (0 if r == 3 else r - 8) + u // 4, 8 + u % 4
-            return OWN, r - (r > 3), u
-        is_shared = (r == 3) | (r > 8)
-        unit = jnp.where(is_shared, 2 * jnp.where(r == 3, 0, r - 8) + u // 4, r - jnp.where(r > 3, 1, 0))
-        return jnp.where(is_shared, SHARED, OWN), unit, jnp.where(is_shared, 8 + u % 4, u)
+            if r in shared_units:
+                return SHARED, shared_units[r][u // 4], 11 - u % 4
+            return OWN, r - (r > 3), 7 - u if r == 8 else u
+        unit = jnp.where(r == 3, shared_units[3][u // 4], r - jnp.where(r > 3, 1, 0))
+        return jnp.where(r == 3, SHARED, OWN), unit, jnp.where(r == 3, 11 - u % 4, u)
+
+    def each(*actions):
+        def run():
+            for action, *arguments in actions:
+                action(*arguments)
+
+        return run
+
+    def q_arrived(*ids):
+        for i in ids:
+            if i < 8:
+                q_own_copy(i).wait_recv()
+            else:
+                q_shared_copy(i - 8).wait_recv()
+
+    def send_shared():
+        for i in range(1, 4):
+            shared_z_copy(i).start()
 
     plan = {
-        (1, 4): lambda: second(SHARED, 1),
-        (1, 7): lambda: arrived(OWN, 2),
-        (2, 0): lambda: own_first(3),
-        (2, 4): lambda: own_first(4),
-        (2, 7): lambda: (arrived(SHARED, 0), arrived(SHARED, 1), [q_shared_copy(i).wait_recv() for i in (1, 2, 3)]),
-        (3, 0): lambda: second(OWN, 3),
-        (3, 4): lambda: second(OWN, 4),
-        (3, 7): lambda: arrived(OWN, 3),
-        (4, 0): lambda: own_first(5),
-        (4, 4): lambda: own_first(6),
-        (4, 7): lambda: arrived(OWN, 4),
-        (5, 0): lambda: second(OWN, 5),
-        (5, 4): lambda: (second(OWN, 6), own_first(7)),
-        (5, 7): lambda: arrived(OWN, 5),
-        (6, 0): lambda: shared_first(2),
-        (6, 4): lambda: second(OWN, 7),
-        (6, 7): lambda: arrived(OWN, 6),
-        (7, 0): lambda: shared_first(4),
-        (7, 4): lambda: (shared_first(6), second(SHARED, 2)),
-        (7, 7): lambda: arrived(OWN, 7),
-        (9, 0): lambda: second(SHARED, 5),
-        (9, 4): lambda: second(SHARED, 7),
-        (9, 7): lambda: (arrived(SHARED, 4), arrived(SHARED, 5)),
-        (10, 7): lambda: (arrived(SHARED, 6), arrived(SHARED, 7)),
+        (0, 0): each((second, OWN, 0), (own_first, 1), (own_first, 2), (arrived, OWN, 0)),
+        (0, 1): each((q_arrived, 1, 2)),
+        (0, 3): each((q_arrived, 3, 4)),
+        (0, 5): each(
+            (q_arrived, 5, 6, 7), (second, OWN, 1), (second, OWN, 2), (second, SHARED, 0), (shared_first, 1)
+        ),
+        (1, 0): each((send_shared,), (arrived, OWN, 1)),
+        (2, 0): each((arrived, OWN, 2), (second, SHARED, 1), (own_first, 3)),
+        (3, 0): each((own_first, 4), (q_arrived, 9, 10, 11), (arrived, SHARED, 0), (arrived, SHARED, 1)),
+        (4, 0): each((second, OWN, 3), (second, OWN, 4), (own_first, 5), (arrived, OWN, 3)),
+        (5, 0): each((own_first, 6), (own_first, 7), (arrived, OWN, 4)),
+        (6, 0): each((second, OWN, 5), (second, OWN, 6), (shared_first, 2), (arrived, OWN, 5)),
+        (7, 0): each((second, OWN, 7), (shared_first, 4), (shared_first, 6), (arrived, OWN, 6)),
+        (8, 0): each((second, SHARED, 2), (arrived, OWN, 7)),
+        (8, 4): each((shared_first, 3), (shared_first, 5), (second, SHARED, 4)),
+        (9, 0): each((second, SHARED, 6), (shared_first, 7), (arrived, SHARED, 2), (arrived, SHARED, 4)),
+        (10, 0): each((second, SHARED, 3), (arrived, SHARED, 6)),
+        (10, 4): each((second, SHARED, 5), (arrived, SHARED, 3)),
+        (11, 0): each((second, SHARED, 7), (arrived, SHARED, 5)),
+        (11, 4): each((arrived, SHARED, 7)),
     }
 
-    def pass_on(r, u):
-        for (at, step), action in plan.items():
-            if step == u:
-                pl.when(r == at)(lambda action=action: (action(), None)[1])
-
-    def round_of_eight(r, carry):
+    def steps(r, before):
         for u in range(8):
-            pass_on(r, u)
-            scores(*(place(r, u + 1) if u < 7 else place(r + 1, 0)), (u + 1) % 2)
-            weigh(*place(r, u), u % 2)
+            if isinstance(r, int):
+                if (r, u) in plan:
+                    plan[r, u]()
+            elif u == 0:
+                for at in range(1, 8):
+                    pl.when(r == at)(plan[at, 0])
+            scores(*place(r, u), u % 2)
+            if u > 0 or before is not None:
+                previous = place(r, u - 1) if u else place(before, 7)
+                weighed(r if u else before, u - 1 if u else 7, weigh(*previous, (u + 1) % 2))
+
+    def weighed(r, u, total):
+        if isinstance(r, int) and (r == 8 or (r == 11 and u >= 4)):
+            finish(place(r, u)[2], total)
+
+    steps(0, None)
+
+    def one_round(r, carry):
+        steps(r, r - 1)
         return carry
 
-    second(OWN, 0)
-    arrived(OWN, 0)
-    scores(OWN, 0, 0, 0)
-    for u in range(8):
-        if u == 2:
-            own_first(1)
-            own_first(2)
-        if u == 4:
-            second(SHARED, 0)
-            shared_first(1)
-        if u == 6:
-            second(OWN, 1)
-            second(OWN, 2)
-        if u < 7:
-            q_own_copy(u + 1).wait_recv()
-            scores(OWN, 0, u + 1, (u + 1) % 2)
-        else:
-            arrived(OWN, 1)
-            scores(OWN, 1, 0, 0)
-        weigh(OWN, 0, u, u % 2)
-
-    lax.fori_loop(1, 8, round_of_eight, 0)
-
-    order = (0, 7, 6, 5, 4, 3, 2, 1)
-    for u, b in enumerate(order):
-        if u == 0:
-            shared_first(3)
-        if u == 2:
-            second(SHARED, 4)
-        if u == 4:
-            shared_first(5)
-            second(SHARED, 6)
-        if u == 6:
-            shared_first(7)
-            second(SHARED, 3)
-        if u < 7:
-            scores(OWN, 7, order[u + 1], (u + 1) % 2)
-        else:
-            arrived(SHARED, 2)
-            arrived(SHARED, 3)
-            scores(SHARED, 2, 8, 0)
-        finish(b, weigh(OWN, 7, b, u % 2))
-
-    lax.fori_loop(9, 11, round_of_eight, 0)
-
-    for u in range(8):
-        if u < 7:
-            scores(*place(11, u + 1), (u + 1) % 2)
-        total = weigh(*place(11, u), u % 2)
-        if u >= 4:
-            finish(4 + u, total)
+    lax.fori_loop(1, 8, one_round, 0)
+    for r in (8, 9, 10, 11):
+        steps(r, r - 1)
+    weighed(11, 7, weigh(*place(11, 7), 1))
 
     for load in loads:
         load.wait()

time: 78.1 us -> 73.3 us (0.939)
  Pallas kernels: 77.3 us -> 72.6 us
    pallas_call x1, Pallas kernels: 75 us -> 70.3 us  [local(): pl.pallas_call(kernel, out_shape=out_shape, in_specs=[hbm, vmem, vmem, vm...]
where the time goes in v3:
time: 73.3 us; the launch traced here: 73.2 us
  Pallas kernels  72.6 us (99%)
    pallas_call x1, Pallas kernels, local(): pl.pallas_call(kernel, out_shape=out_shape, in_specs=[hbm, vmem, vmem, vm...  70.3 us
    pallas_call x1, Pallas kernels, local(): pl.pallas_call(hand_on, out_shape=out_shape, in_specs=[vmem, vmem], out_s...  2.29 us

profile of v3, /device:TPU:1, one launch (start us, length us, event | category | flops | bytes accessed | tf_op | source)
XLA Modules:
  0.0 73.2 jit_solution(4942880816600036155)
XLA Ops:
  0.6 70.3 %shard_map.113 = (bf16[256,1536]{1,0:T(8,128)(2,1)}, bf16[256,768]{1,0:T(8,128)(2,1)}) custom-call(bf16[256,1536]{1,0:T(8,128)(2,1)} %frames_hbm.1, bf16[256,768]{1,0:T(8,128)(2,1)} %q_ref.1, bf16[256,768]{1,0:T(8,128)(2,1)} %k_ref.1, bf16[256,768]{1,0:T(8,128)(2,1)} %v_ref.1, bf16[768,1536]{1,0:T(8,128)(2,1)} %wout_hbm.1, f32[1536]{0:T(1024)} %gain_ref.1, ...), custom_call_target="tpu_custom_call" | custom-call | tf_op jit(solution)/shard_map/pallas_call | solution.py:398
  70.9 2.3 %shard_map.114 = (bf16[256,1536]{1,0:T(8,128)(2,1)}, bf16[256,768]{1,0:T(8,128)(2,1)}) custom-call(bf16[256,1536]{1,0:T(8,128)(2,1)} %get-tuple-element.4.att_in, bf16[256,768]{1,0:T(8,128)(2,1)} %get-tuple-element.5.conv_in), custom_call_target="tpu_custom_call" | custom-call | tf_op jit(solution)/shard_map/pallas_call | solution.py:431

commit v4 on v3

--- a/solution.py
+++ b/solution.py
@@ -25,8 +25,9 @@
 
 
 def kernel(
-    frames_hbm, q_ref, k_ref, v_ref, wout_hbm, gain_ref, wglu_hbm, dw_ref, bns_ref, bnb_ref,
-    att_ref, conv_ref,
+    frames_hbm, q_hbm, k_hbm, v_hbm, wout_hbm, gain_hbm, wglu_hbm, dw_hbm, bns_hbm, bnb_hbm,
+    att_hbm, conv_hbm,
+    q_ref, k_ref, v_ref, gain_ref, dw_ref, bns_ref, bnb_ref, att_ref, conv_ref,
     kv_send, q_send, kv, qb, ctx_send, ctx_t, s_scr, mx_scr, m_scr, acc_scr,
     frames, wout, wglu, gpad, taps_tmp, halo_send, halo_recv,
     local_sem, q_ssem, q_rsem, z_ssem, z_rsem, a_ssem, a_rsem, x_ssem, x_rsem, b_ssem, b_rsem,
@@ -60,13 +61,15 @@
     for peer in peers:
         pl.semaphore_signal(barrier, inc=1, device_id=peer, device_id_type=MESH)
 
-    loads = [
-        pltpu.make_async_copy(frames_hbm, frames, local_sem.at[0]),
-        pltpu.make_async_copy(wout_hbm, wout, local_sem.at[1]),
-        pltpu.make_async_copy(wglu_hbm, wglu, local_sem.at[2]),
+    pairs = [
+        (q_hbm, q_ref), (v_hbm, v_ref), (k_hbm, k_ref), (frames_hbm, frames), (wout_hbm, wout), (wglu_hbm, wglu),
+        (gain_hbm, gain_ref), (dw_hbm, dw_ref), (bns_hbm, bns_ref), (bnb_hbm, bnb_ref),
     ]
+    loads = [pltpu.make_async_copy(src, dst, local_sem.at[i]) for i, (src, dst) in enumerate(pairs)]
     for load in loads:
         load.start()
+    for load in loads[:3]:
+        load.wait()
 
     q_send[...] = q_ref[...].T.reshape(q_send.shape)
     v_t = v_ref[...].T
@@ -302,7 +305,7 @@
         steps(r, r - 1)
     weighed(11, 7, weigh(*place(11, 7), 1))
 
-    for load in loads:
+    for load in loads[3:]:
         load.wait()
 
     def project(heads):
@@ -317,6 +320,8 @@
         context_copy(b).wait_recv()
     residual = residual + project(SHARED_HEADS)
     att_ref[...] = residual.astype(BF16)
+    att_store = pltpu.make_async_copy(att_ref, att_hbm, local_sem.at[0])
+    att_store.start()
     centered = residual - jnp.mean(residual, axis=1, keepdims=True)
     variance = jnp.mean(centered * centered, axis=1, keepdims=True)
     gain = gain_ref[...].reshape(1, -1)
@@ -352,13 +357,22 @@
             u = bn_scale[:, cols] * conv + bn_shift[:, cols]
             conv_ref[first : first + rows, cols] = (u * jax.nn.sigmoid(u)).astype(BF16)
 
+    def store(first, rows, sem):
+        part = pl.ds(first, rows)
+        return pltpu.make_async_copy(conv_ref.at[part], conv_hbm.at[part], local_sem.at[sem])
+
     convolve(EDGE, ROWS - 2 * EDGE)
+    inner_store = store(EDGE, ROWS - 2 * EDGE, 1)
+    inner_store.start()
     to_left.wait_recv()
     to_right.wait_recv()
     gpad[:EDGE, :] = jnp.where(me == 0, 0.0, halo_recv[0].astype(F32))
     gpad[EDGE + ROWS :, :] = jnp.where(me == 31, 0.0, halo_recv[1].astype(F32))
     convolve(0, EDGE)
     convolve(ROWS - EDGE, EDGE)
+    edge_stores = [store(0, EDGE, 2), store(ROWS - EDGE, EDGE, 3)]
+    for edge in edge_stores:
+        edge.start()
 
     for n in range(1, Z):
         q_own_copy(n).wait_send()
@@ -378,17 +392,35 @@
             context_copy(b).wait_send()
     to_left.wait_send()
     to_right.wait_send()
-
-
-def hand_on(att_in, conv_in, att_out, conv_out):
-    att_out[...] = att_in[...]
-    conv_out[...] = conv_in[...]
+    for copy in [att_store, inner_store] + edge_stores:
+        copy.wait()
+
+
+def hand_on(att_in, conv_in, att_out, conv_out, att, conv, in_sem, out_sem):
+    rows = ROWS // 4
+    copies = []
+    for i in range(4):
+        part = pl.ds(i * rows, rows)
+        for j, (src, held, dst) in enumerate([(att_in, att, att_out), (conv_in, conv, conv_out)]):
+            copies.append(
+                (
+                    pltpu.make_async_copy(src.at[part], held.at[part], in_sem.at[2 * i + j]),
+                    pltpu.make_async_copy(held.at[part], dst.at[part], out_sem.at[2 * i + j]),
+                )
+            )
+    for load, store in copies:
+        load.start()
+    for load, store in copies:
+        load.wait()
+        store.start()
+    for load, store in copies:
+        store.wait()
 
 
 def local(frames_in, queries, keys, values, w_out, ln_gain, w_glu, dw_weight, bn_scale, bn_shift):
     rows, width = frames_in.shape
     channels = w_glu.shape[1] // 2
-    vmem, hbm = pl.BlockSpec(memory_space=pltpu.VMEM), pl.BlockSpec(memory_space=pl.ANY)
+    hbm = pl.BlockSpec(memory_space=pl.ANY)
     dma = pltpu.SemaphoreType.DMA
     units = [dma((2, Z))] * 8
     out_shape = (
@@ -398,9 +430,18 @@
     results = pl.pallas_call(
         kernel,
         out_shape=out_shape,
-        in_specs=[hbm, vmem, vmem, vmem, hbm, vmem, hbm, vmem, vmem, vmem],
-        out_specs=(vmem, vmem),
+        in_specs=[hbm] * 10,
+        out_specs=(hbm, hbm),
         scratch_shapes=[
+            pltpu.VMEM(queries.shape, BF16),
+            pltpu.VMEM(keys.shape, BF16),
+            pltpu.VMEM(values.shape, BF16),
+            pltpu.VMEM(ln_gain.shape, F32),
+            pltpu.VMEM(dw_weight.shape, F32),
+            pltpu.VMEM(bn_scale.shape, F32),
+            pltpu.VMEM(bn_shift.shape, F32),
+            pltpu.VMEM((rows, width), BF16),
+            pltpu.VMEM((rows, channels), BF16),
             pltpu.VMEM((12, ROWS, 128), BF16),
             pltpu.VMEM((12, HD, ROWS), BF16),
             pltpu.VMEM((2, Z, 4, ROWS, 128), BF16),
@@ -418,7 +459,7 @@
             pltpu.VMEM((8, ROWS + 8, 128), F32),
             pltpu.VMEM((2, EDGE, channels), BF16),
             pltpu.VMEM((2, EDGE, channels), BF16),
-            dma((3,)),
+            dma((10,)),
             dma((12,)),
             dma((12,)),
         ]
@@ -431,8 +472,14 @@
     return pl.pallas_call(
         hand_on,
         out_shape=out_shape,
-        in_specs=[vmem, vmem],
-        out_specs=(vmem, vmem),
+        in_specs=[hbm, hbm],
+        out_specs=(hbm, hbm),
+        scratch_shapes=[
+            pltpu.VMEM((rows, width), BF16),
+            pltpu.VMEM((rows, channels), BF16),
+            dma((8,)),
+            dma((8,)),
+        ],
     )(*results)
 
 

time: 73.3 us -> 70 us (0.955)
  Pallas kernels: 72.6 us -> 69.1 us
    pallas_call x2, Pallas kernels: 72.6 us -> 69.1 us  [the longest x1 66.9 us: local(): pl.pallas_call(kernel, out_shape=out_shape, in_specs=[hbm] * 10, out_spec...]
where the time goes in v4:
time: 70 us; the launch traced here: 69.9 us
  Pallas kernels  69.1 us (99%)
  between operations  0.8 us (1%)
    pallas_call x1, Pallas kernels, local(): pl.pallas_call(kernel, out_shape=out_shape, in_specs=[hbm] * 10, out_spec...  66.9 us
    pallas_call x1, Pallas kernels, local(): pl.pallas_call(hand_on, out_shape=out_shape, in_specs=[hbm, hbm], out_spe...  2.16 us

profile of v4, /device:TPU:1, one launch (start us, length us, event | category | flops | bytes accessed | tf_op | source)
XLA Modules:
  0.0 69.9 jit_solution(3431953788151394710)
XLA Ops:
  0.6 66.9 %shard_map.113 = (bf16[256,1536]{1,0:T(8,128)(2,1)}, bf16[256,768]{1,0:T(8,128)(2,1)}) custom-call(bf16[256,1536]{1,0:T(8,128)(2,1)} %frames_hbm.1, bf16[256,768]{1,0:T(8,128)(2,1)} %q_hbm.1, bf16[256,768]{1,0:T(8,128)(2,1)} %k_hbm.1, bf16[256,768]{1,0:T(8,128)(2,1)} %v_hbm.1, bf16[768,1536]{1,0:T(8,128)(2,1)} %wout_hbm.1, f32[1536]{0:T(1024)} %gain_hbm.1, ...), custom_call_target="tpu_custom_call" | custom-call | tf_op jit(solution)/shard_map/pallas_call | solution.py:430
  67.6 2.2 %shard_map.114 = (bf16[256,1536]{1,0:T(8,128)(2,1)}, bf16[256,768]{1,0:T(8,128)(2,1)}) custom-call(bf16[256,1536]{1,0:T(8,128)(2,1)} %get-tuple-element.4.att_in, bf16[256,768]{1,0:T(8,128)(2,1)} %get-tuple-element.5.conv_in), custom_call_target="tpu_custom_call" | custom-call | tf_op jit(solution)/shard_map/pallas_call | solution.py:472

commit v5 on v4

--- a/solution.py
+++ b/solution.py
@@ -57,7 +57,7 @@
         )
 
     barrier = pltpu.get_barrier_semaphore()
-    peers = [dev(x, along_z(d), c) for d in range(1, Z)] + [sibling, across, other]
+    peers = [dev(x, along_z(d), c) for d in (4, 3, 5, 2, 6, 1, 7)] + [sibling, across, other]
     for peer in peers:
         pl.semaphore_signal(barrier, inc=1, device_id=peer, device_id_type=MESH)
 
@@ -66,7 +66,7 @@
         (gain_hbm, gain_ref), (dw_hbm, dw_ref), (bns_hbm, bns_ref), (bnb_hbm, bnb_ref),
     ]
     loads = [pltpu.make_async_copy(src, dst, local_sem.at[i]) for i, (src, dst) in enumerate(pairs)]
-    for load in loads:
+    for load in loads[:3]:
         load.start()
     for load in loads[:3]:
         load.wait()
@@ -175,6 +175,9 @@
         q_shared_copy(i).start()
     for n in (5, 6, 7):
         own_z_copy(n, STEPS[n]).start()
+
+    for load in loads[3:]:
+        load.start()
 
     acc_scr[...] = jnp.zeros_like(acc_scr)
     m_scr[...] = jnp.full_like(m_scr, -1e30)
@@ -326,9 +329,13 @@
     variance = jnp.mean(centered * centered, axis=1, keepdims=True)
     gain = gain_ref[...].reshape(1, -1)
     normed = (centered * lax.rsqrt(variance + 1e-05) * gain).astype(BF16)
-    projected = jnp.dot(normed, wglu[...], preferred_element_type=F32)
-    channels = projected.shape[1] // 2
-    gated = (projected[:, :channels] * jax.nn.sigmoid(projected[:, channels:])).astype(BF16)
+    channels = wglu.shape[1] // 2
+    gated = []
+    for col in range(0, channels, 256):
+        value = jnp.dot(normed, wglu[:, col : col + 256], preferred_element_type=F32)
+        gate = jnp.dot(normed, wglu[:, channels + col : channels + col + 256], preferred_element_type=F32)
+        gated.append((value * jax.nn.sigmoid(gate)).astype(BF16))
+    gated = jnp.concatenate(gated, axis=1)
 
     halo_send[0] = gated[:EDGE]
     halo_send[1] = gated[ROWS - EDGE :]
@@ -351,8 +358,9 @@
                     begin = first + u - r
                     term = gpad[begin : begin + rows + 8, cols] * dw_ref[u - 1 : u, cols]
                     part = term if part is None else part + term
-                taps_tmp[r, : rows + 8] = part
-                shifted = taps_tmp[r, r : r + rows, :]
+                held = taps_tmp.at[col // 128, r]
+                held[first : first + rows + 8, :] = part
+                shifted = held[first + r : first + r + rows, :]
                 conv = shifted if conv is None else conv + shifted
             u = bn_scale[:, cols] * conv + bn_shift[:, cols]
             conv_ref[first : first + rows, cols] = (u * jax.nn.sigmoid(u)).astype(BF16)
@@ -456,7 +464,7 @@
             pltpu.VMEM(w_out.shape, BF16),
             pltpu.VMEM(w_glu.shape, BF16),
             pltpu.VMEM((ROWS + 2 * EDGE, channels), F32),
-            pltpu.VMEM((8, ROWS + 8, 128), F32),
+            pltpu.VMEM((channels // 128, 8, ROWS + 8, 128), F32),
             pltpu.VMEM((2, EDGE, channels), BF16),
             pltpu.VMEM((2, EDGE, channels), BF16),
             dma((10,)),

time: 70 us -> 70 us (level)
  no operation moved by 1% of the time
where the time goes in v5:
time: 70 us; the launch traced here: 69.9 us
  Pallas kernels  69 us (99%)
  between operations  0.8 us (1%)
    pallas_call x1, Pallas kernels, local(): pl.pallas_call(kernel, out_shape=out_shape, in_specs=[hbm] * 10, out_spec...  66.9 us
    pallas_call x1, Pallas kernels, local(): pl.pallas_call(hand_on, out_shape=out_shape, in_specs=[hbm, hbm], out_spe...  2.16 us

profile of v5, /device:TPU:1, one launch (start us, length us, event | category | flops | bytes accessed | tf_op | source)
XLA Modules:
  0.0 69.9 jit_solution(6419838663420291235)
XLA Ops:
  0.6 66.9 %shard_map.113 = (bf16[256,1536]{1,0:T(8,128)(2,1)}, bf16[256,768]{1,0:T(8,128)(2,1)}) custom-call(bf16[256,1536]{1,0:T(8,128)(2,1)} %frames_hbm.1, bf16[256,768]{1,0:T(8,128)(2,1)} %q_hbm.1, bf16[256,768]{1,0:T(8,128)(2,1)} %k_hbm.1, bf16[256,768]{1,0:T(8,128)(2,1)} %v_hbm.1, bf16[768,1536]{1,0:T(8,128)(2,1)} %wout_hbm.1, f32[1536]{0:T(1024)} %gain_hbm.1, ...), custom_call_target="tpu_custom_call" | custom-call | tf_op jit(solution)/shard_map/pallas_call | solution.py:438
  67.5 2.2 %shard_map.114 = (bf16[256,1536]{1,0:T(8,128)(2,1)}, bf16[256,768]{1,0:T(8,128)(2,1)}) custom-call(bf16[256,1536]{1,0:T(8,128)(2,1)} %get-tuple-element.4.att_in, bf16[256,768]{1,0:T(8,128)(2,1)} %get-tuple-element.5.conv_in), custom_call_target="tpu_custom_call" | custom-call | tf_op jit(solution)/shard_map/pallas_call | solution.py:480
